TPU v7x, 32 devices: a whole 2x2x4 slice. The times are simulated.
32 devices in a mesh: dp: 8 (over y, x, core), seq: 4 (over z).
Axes of the slice: x: 2, y: 2, z: 4, core: 2. Of those that a mesh axis runs over, the one named last changes fastest.
Arguments:
- tokens: bfloat16 [96, 320, 768], P('dp', 'seq'), may hold values from -6 to 6
- lengths: int32 [96], P('dp'), may hold values from 197 to 577, as said below
- grad_out: bfloat16 [96, 320, 768], P('dp', 'seq'), may hold values from -6 to 6
- query_weight: bfloat16 [768, 768], replicated, may hold values from -0.4375 to 0.4375
- query_bias: bfloat16 [768], replicated, may hold values from -1.796875 to 1.796875
- key_weight: bfloat16 [768, 768], replicated, may hold values from -0.21875 to 0.21875
- value_weight: bfloat16 [768, 768], replicated, may hold values from -0.21875 to 0.21875
- value_bias: bfloat16 [768], replicated, may hold values from -1.796875 to 1.796875
- output_weight: bfloat16 [768, 768], replicated, may hold values from -0.875 to 0.875
- output_bias: bfloat16 [768], replicated, may hold values from -1.796875 to 1.796875
- up_weight: bfloat16 [768, 3072], replicated, may hold values from -0.21875 to 0.21875
- up_bias: bfloat16 [3072], replicated, may hold values from -1.796875 to 1.796875
- down_weight: bfloat16 [3072, 768], replicated, may hold values from -0.21875 to 0.21875
- down_bias: bfloat16 [768], replicated, may hold values from -1.796875 to 1.796875
- first_gain: bfloat16 [768], replicated, may hold values from 0.5 to 1.5
- first_shift: bfloat16 [768], replicated, may hold values from -1.796875 to 1.796875
- second_gain: bfloat16 [768], replicated, may hold values from 0.5 to 1.5
- second_shift: bfloat16 [768], replicated, may hold values from -1.796875 to 1.796875
- router_weight: bfloat16 [768], replicated, may hold values from -0.21875 to 0.21875
Outputs:
- mixed: bfloat16 [96, 320, 768], P('dp', 'seq')
- tokens_grad: bfloat16 [96, 320, 768], P('dp', 'seq')
- grad_query_weight: float32 [768, 768], replicated
- grad_query_bias: float32 [768], replicated
- grad_key_weight: float32 [768, 768], replicated
- grad_value_weight: float32 [768, 768], replicated
- grad_value_bias: float32 [768], replicated
- grad_output_weight: float32 [768, 768], replicated
- grad_output_bias: float32 [768], replicated
- grad_up_weight: float32 [768, 3072], replicated
- grad_up_bias: float32 [3072], replicated
- grad_down_weight: float32 [3072, 768], replicated
- grad_down_bias: float32 [768], replicated
- grad_first_gain: float32 [768], replicated
- grad_first_shift: float32 [768], replicated
- grad_second_gain: float32 [768], replicated
- grad_second_shift: float32 [768], replicated
- grad_router_weight: float32 [768], replicated
Inputs may be any that keep to these rules, and one draw needn't show every extreme that they name: `lengths`: each length is 197 or 577; each run of 12 images of one dp index holds at least one of length 577.
All inputs are finite; a program needn't handle non-finite values.
Results may differ from a plain program's by a relative error of at most 0.019.
Values may be sent and summed in bfloat16 or wider, within the bound.
No kernel may reach another device: no remote copies, remote signals or barrier semaphores. Data moves between devices by JAX's collectives and lax.ppermute only.
A program may use at most 256 MiB of HBM per device.

v0:
```python
from functools import partial

import jax
import jax.numpy as jnp
from jax import lax
from jax.sharding import PartitionSpec as P

HEADS = 12
HEAD_DIM = 64


EPSILON = 1e-06


def normalize(field, gain, shift):
    middle = jnp.mean(field, axis=-1, keepdims=True)
    centred = field - middle
    spread = jnp.mean(centred * centred, axis=-1, keepdims=True)
    return centred * lax.rsqrt(spread + EPSILON) * gain + shift


def project(left, right):
    return jnp.einsum("icn,no->ico", left, right, preferred_element_type=jnp.float32)


def back_project(grad, weight):
    return jnp.einsum("ico,no->icn", grad, weight, preferred_element_type=jnp.float32)


def outer_sum(left, right):
    return jnp.einsum("icn,ico->no", left, right, preferred_element_type=jnp.float32)


def column_sum(grad):
    return jnp.sum(grad.astype(jnp.float32), axis=(0, 1))


def split_heads(field):
    return field.reshape(field.shape[0], field.shape[1], HEADS, HEAD_DIM)


def scores_of(queries, keys_all, key_valid):
    raw = jnp.einsum(
        "iqhe,ikhe->ihqk",
        split_heads(queries),
        split_heads(keys_all),
        preferred_element_type=jnp.float32,
    ) * HEAD_DIM ** (-0.5)
    return jnp.where(key_valid[:, None, None, :] > 0, raw, -1e30)


def on_device(
    tokens,
    lengths,
    grad_out,
    query_weight,
    query_bias,
    key_weight,
    value_weight,
    value_bias,
    output_weight,
    output_bias,
    up_weight,
    up_bias,
    down_weight,
    down_bias,
    first_gain,
    first_shift,
    second_gain,
    second_shift,
    router_weight,
):
    images, slots, width = tokens.shape
    total_slots = slots * lax.axis_size("seq")
    counts = (lengths + 1) // 2
    own_slot = lax.axis_index("seq") * slots + jnp.arange(slots, dtype=jnp.int32)
    valid = (own_slot[None, :] < counts[:, None]).astype(jnp.float32)
    key_valid = (jnp.arange(total_slots, dtype=jnp.int32)[None, :] < counts[:, None]).astype(
        jnp.float32
    )
    router_float = router_weight.astype(jnp.float32)
    inputs = tokens.astype(jnp.float32)
    first_norm, first_pull = jax.vjp(
        normalize, inputs, first_gain.astype(jnp.float32), first_shift.astype(jnp.float32)
    )
    normed = first_norm.astype(jnp.bfloat16)
    gate = jax.nn.sigmoid(
        jnp.einsum("icd,d->ic", normed, router_weight, preferred_element_type=jnp.float32)
    )
    weight_row = valid * gate
    queries = (project(normed, query_weight) + query_bias.astype(jnp.float32)).astype(jnp.bfloat16)
    keys_local = project(normed, key_weight).astype(jnp.bfloat16)
    values_local = (project(normed, value_weight) + value_bias.astype(jnp.float32)).astype(
        jnp.bfloat16
    )
    keys_all, values_all = (
        lax.all_gather(keys_local, "seq", axis=1, tiled=True),
        lax.all_gather(values_local, "seq", axis=1, tiled=True),
    )
    scores = scores_of(queries, keys_all, key_valid)
    top = jnp.max(scores, axis=-1, keepdims=True)
    expo = jnp.exp(scores - top)
    total = jnp.sum(expo, axis=-1, keepdims=True)
    log_total = top + jnp.log(total)
    probs_low = (expo / total).astype(jnp.bfloat16)
    context = jnp.einsum(
        "ihqk,ikhe->iqhe", probs_low, split_heads(values_all), preferred_element_type=jnp.float32
    ).reshape(images, slots, width)
    context_low = context.astype(jnp.bfloat16)
    branch_one = project(context_low, output_weight) + output_bias.astype(jnp.float32)
    middle = inputs + weight_row[..., None] * branch_one
    second_norm, second_pull = jax.vjp(
        normalize, middle, second_gain.astype(jnp.float32), second_shift.astype(jnp.float32)
    )
    second_low = second_norm.astype(jnp.bfloat16)
    hidden = project(second_low, up_weight) + up_bias.astype(jnp.float32)
    activated, gelu_pull = jax.vjp(partial(jax.nn.gelu, approximate=False), hidden)
    activated_low = activated.astype(jnp.bfloat16)
    branch_two = project(activated_low, down_weight) + down_bias.astype(jnp.float32)
    mixed = (middle + weight_row[..., None] * branch_two).astype(jnp.bfloat16)
    upstream = grad_out.astype(jnp.float32)
    grad_branch_two = (weight_row[..., None] * upstream).astype(jnp.bfloat16)
    grad_down_bias = column_sum(grad_branch_two)
    grad_down_weight = outer_sum(activated_low, grad_branch_two)
    (grad_hidden,) = gelu_pull(back_project(grad_branch_two, down_weight))
    grad_hidden_low = grad_hidden.astype(jnp.bfloat16)
    grad_up_bias = column_sum(grad_hidden_low)
    grad_up_weight = outer_sum(second_low, grad_hidden_low)
    grad_middle, grad_second_gain, grad_second_shift = second_pull(
        back_project(grad_hidden_low, up_weight)
    )
    grad_middle = grad_middle + upstream
    grad_gate_row = valid * (
        jnp.sum(upstream * branch_two, axis=-1) + jnp.sum(grad_middle * branch_one, axis=-1)
    )
    grad_branch_one = (weight_row[..., None] * grad_middle).astype(jnp.bfloat16)
    grad_output_bias = column_sum(grad_branch_one)
    grad_output_weight = outer_sum(context_low, grad_branch_one)
    grad_context = back_project(grad_branch_one, output_weight).astype(jnp.bfloat16)
    keys_back, values_back = (
        lax.all_gather(keys_local, "seq", axis=1, tiled=True),
        lax.all_gather(values_local, "seq", axis=1, tiled=True),
    )
    probs_again = jnp.exp(scores_of(queries, keys_back, key_valid) - log_total)
    grad_probs = jnp.einsum(
        "iqhe,ikhe->ihqk",
        split_heads(grad_context),
        split_heads(values_back),
        preferred_element_type=jnp.float32,
    )
    centre = jnp.sum(probs_again * grad_probs, axis=-1, keepdims=True)
    grad_scores = (probs_again * (grad_probs - centre)).astype(jnp.bfloat16)
    scale = HEAD_DIM ** (-0.5)
    grad_queries = (
        jnp.einsum(
            "ihqk,ikhe->iqhe",
            grad_scores,
            split_heads(keys_back),
            preferred_element_type=jnp.float32,
        )
        * scale
    ).reshape(images, slots, width)
    grad_queries = grad_queries.astype(jnp.bfloat16)
    grad_keys_term = (
        jnp.einsum(
            "ihqk,iqhe->ikhe", grad_scores, split_heads(queries), preferred_element_type=jnp.float32
        )
        * scale
    ).reshape(images, total_slots, width)
    grad_values_term = jnp.einsum(
        "ihqk,iqhe->ikhe",
        probs_again.astype(jnp.bfloat16),
        split_heads(grad_context),
        preferred_element_type=jnp.float32,
    ).reshape(images, total_slots, width)
    grad_keys_own, grad_values_own = (
        lax.psum_scatter(
            grad_keys_term.astype(jnp.bfloat16), "seq", scatter_dimension=1, tiled=True
        ).astype(jnp.float32),
        lax.psum_scatter(
            grad_values_term.astype(jnp.bfloat16), "seq", scatter_dimension=1, tiled=True
        ).astype(jnp.float32),
    )
    grad_keys_low = grad_keys_own.astype(jnp.bfloat16)
    grad_values_low = grad_values_own.astype(jnp.bfloat16)
    grad_query_bias = column_sum(grad_queries)
    grad_value_bias = column_sum(grad_values_low)
    grad_query_weight = outer_sum(normed, grad_queries)
    grad_key_weight = outer_sum(normed, grad_keys_low)
    grad_value_weight = outer_sum(normed, grad_values_low)
    grad_logit = grad_gate_row * gate * (1.0 - gate)
    grad_router_weight = jnp.einsum(
        "icd,ic->d", normed, grad_logit, preferred_element_type=jnp.float32
    )
    grad_normed = (
        back_project(grad_queries, query_weight)
        + back_project(grad_keys_low, key_weight)
        + back_project(grad_values_low, value_weight)
        + grad_logit[..., None] * router_float
    )
    grad_inputs, grad_first_gain, grad_first_shift = first_pull(grad_normed)
    tokens_grad = (grad_inputs + grad_middle).astype(jnp.bfloat16)
    pieces = [
        grad_query_weight,
        grad_query_bias,
        grad_key_weight,
        grad_value_weight,
        grad_value_bias,
        grad_output_weight,
        grad_output_bias,
        grad_up_weight,
        grad_up_bias,
        grad_down_weight,
        grad_down_bias,
        grad_first_gain,
        grad_first_shift,
        grad_second_gain,
        grad_second_shift,
        grad_router_weight,
    ]
    flat = jnp.concatenate([piece.reshape(-1) for piece in pieces])
    devices = lax.axis_size("dp") * lax.axis_size("seq")
    block = devices * 128
    padded_length = -(-flat.shape[0] // block) * block
    leading = padded_length - flat.shape[0]
    flat = jnp.pad(flat, (leading, 0)).reshape(padded_length // 128, 128)
    share = lax.psum_scatter(
        flat.astype(jnp.bfloat16), "seq", scatter_dimension=0, tiled=True
    ).astype(jnp.float32)
    share = lax.psum_scatter(share, "dp", scatter_dimension=0, tiled=True)
    share = lax.all_gather(share.astype(jnp.bfloat16), "dp", axis=0, tiled=True).astype(share.dtype)
    summed = lax.all_gather(share.astype(jnp.bfloat16), "seq", axis=0, tiled=True).astype(
        share.dtype
    )
    summed = summed.reshape(-1)
    results = []
    offset = leading
    for piece in pieces:
        results.append(summed[offset : offset + piece.size].reshape(piece.shape))
        offset = offset + piece.size
    return (
        mixed,
        tokens_grad,
        results[0],
        results[1],
        results[2],
        results[3],
        results[4],
        results[5],
        results[6],
        results[7],
        results[8],
        results[9],
        results[10],
        results[11],
        results[12],
        results[13],
        results[14],
        results[15],
    )


def solution(mesh):
    in_specs = (
        P("dp", "seq", None),
        P("dp"),
        P("dp", "seq", None),
        P(),
        P(),
        P(),
        P(),
        P(),
        P(),
        P(),
        P(),
        P(),
        P(),
        P(),
        P(),
        P(),
        P(),
        P(),
        P(),
    )
    out_specs = (
        P("dp", "seq", None),
        P("dp", "seq", None),
        P(),
        P(),
        P(),
        P(),
        P(),
        P(),
        P(),
        P(),
        P(),
        P(),
        P(),
        P(),
        P(),
        P(),
        P(),
        P(),
    )
    return jax.shard_map(
        on_device, mesh=mesh, in_specs=in_specs, out_specs=out_specs, check_vma=False
    )
```

profile of v0, /device:TPU:0, one launch (start us, length us, event | category | flops | bytes accessed | tf_op | source)
XLA Modules:
  0.0 1498.4 jit_solution(4330548445610674948)
XLA Ops:
  13.1 2.7 convolution_convert_fusion.1
  16.0 4.0 add_convert_fusion.5
  20.4 3.9 add_convert_fusion.4
  24.3 4.0 copy.62
  29.3 98.2 %all-gather.8.cloned.1.call-done = bf16[12,320,768]{2,1,0:T(8,128)(2,1)} async-done(((bf16[12,80,768]{2,1,0:T(8,128)(2,1)}), bf16[12,320,768]{2,1,0:T(8,128)(2,1)}) %all-gather.8.cloned.1.call-update) | async-done | bytes 5898256 | tf_op jit(solution)/shard_map/all_gather | solution.py:97
  127.6 9.5 copy.63
  137.1 13.3 fusion.80
  150.4 8.5 fusion.1
  159.5 77.3 %all-gather.6.cloned.1.call-done = bf16[12,320,768]{2,1,0:T(8,128)(2,1)} async-done(((bf16[12,80,768]{2,1,0:T(8,128)(2,1)}), bf16[12,320,768]{2,1,0:T(8,128)(2,1)}) %all-gather.6.cloned.1.call-update) | async-done | bytes 5898256 | tf_op jit(solution)/shard_map/all_gather | solution.py:98
  236.8 9.5 copy.61
  246.3 11.4 fusion.39
  257.8 5.2 fusion.77
  263.5 7.6 fusion.17
  271.2 28.2 %multiply_convert_fusion.2 = (bf16[12,80,3072]{2,1,0:T(8,128)(2,1)}, f32[12,80,3072]{2,1,0:T(8,128)}) fusion(f32[12,80,3072]{2,1,0:T(8,128)S(1)} %get-tuple-element.57, f32[3072]{0:T(1024)S(1)} %convert_element_type.183, u16[80,3072]{1,0:T(8,128)(2,1)S(1)} %get-tuple-element.19, u16[80,3072]{1,0:T(8,128)(2,1)S(1)} %get-tuple-element.18), kind=kLoop, calls=%fused_computation.18 | loop fusion | flops 209387520 | bytes 30486528 | tf_op jit(solution)/shard_map/convert_element_type | solution.py:118
  299.4 18.8 %fusion.82 = (bf16[3072]{0:T(1024)(128)(2,1)}, bf16[12,80,3072]{2,1,0:T(8,128)(2,1)}) fusion(f32[12,80,3072]{2,1,0:T(8,128)} %get-tuple-element.34, bf16[3072,768]{1,0:T(8,128)(2,1)} %param.31, bf16[12,80,768]{2,1,0:T(8,128)(2,1)} %param.21, f32[12,80]{1,0:T(8,128)S(1)} %compare_select_fusion.1, f32[12,80,3072]{2,1,0:T(8,128)} %copy-done.12, ...), kind=kOutput, calls=%fused_computation.151 | convolution fusion | flops 4579243008 | bytes 35706624 | tf_op jit(solution)/shard_map/ico,no->icn/dot_general | solution.py:27
  318.3 9.4 multiply_reduce_fusion.1
  331.7 2.5 convolution_convert_fusion
  334.1 2.9 copy.65
  337.0 9.4 fusion.13
  346.4 9.3 copy.68
  357.6 15.8 %multiply_reduce_fusion = (f32[12,12,80]{2,1,0:T(8,128)S(1)}, f32[12,12,80,320]{3,2,1,0:T(8,128)}) fusion(f32[12,12,80,320]{3,2,1,0:T(8,128)} %get-tuple-element.55, f32[12,12,80]{2,1,0:T(8,128)S(1)} %copy-done.20, bf16[12,80,12,64]{1,3,2,0:T(8,128)(2,1)S(1)} %bitcast.148, bf16[12,320,12,64]{1,3,2,0:T(8,128)(2,1)} %bitcast.150), kind=kOutput, calls=%fused_computation.1 | convolution fusion | flops 482906880 | bytes 36956160 | tf_op jit(solution)/shard_map/iqhe,ikhe->ihqk/dot_general | solution.py:145
  373.4 12.5 multiply_convert_fusion
  385.9 4.7 multiply_convert_fusion.1
  391.6 9.4 copy.67
  401.0 10.9 fusion.81
  411.9 10.1 bitcast_convert_fusion
  422.0 10.1 fusion.38
  433.8 4.1 bitcast_convert_fusion.2
  437.9 3.6 copy.77
  441.6 9.3 reshape.246
  450.9 2.6 reshape.244
  453.6 5.2 bitcast_convert_fusion.5
  458.8 3.4 reshape.241
  462.2 2.4 constant_dynamic-update-slice_fusion.1
  466.3 14.3 multiply_reduce_fusion.2
  482.7 3.7 fusion.46
  486.4 4.2 bitcast_convert_fusion.3
  490.6 3.3 reshape.243
  493.9 71.6 %reduce-scatter.8.cloned.1.call-done = bf16[12,80,768]{2,1,0:T(8,128)(2,1)} async-done(((bf16[12,320,768]{2,1,0:T(8,128)(2,1)}), bf16[12,80,768]{2,1,0:T(8,128)(2,1)}) %reduce-scatter.8.cloned.1.call-update) | async-done | bytes 1474576 | tf_op jit(solution)/shard_map/reduce_scatter | solution.py:177
  565.6 4.1 bitcast_convert_fusion.4
  569.7 3.5 reshape.242
  573.3 3.2 fusion.43
  581.6 19.2 %dynamic-update-slice.2 = bf16[7087872]{0:T(1024)(128)(2,1)} dynamic-update-slice(bf16[7087872]{0:T(1024)(128)(2,1)} %dynamic-update-slice.1, bf16[589824]{0:T(1024)(128)(2,1)} %reshape.242, s32[]{} %constant.135) | dynamic-update-slice | bytes 2359300
  600.8 19.2 %dynamic-update-slice.3 = bf16[7087872]{0:T(1024)(128)(2,1)} dynamic-update-slice(bf16[7087872]{0:T(1024)(128)(2,1)} %dynamic-update-slice.2, bf16[589824]{0:T(1024)(128)(2,1)} %reshape.243, s32[]{} %constant.136) | dynamic-update-slice | bytes 2359300
  623.0 18.9 %dynamic-update-slice.5 = bf16[7087872]{0:T(1024)(128)(2,1)} dynamic-update-slice(bf16[7087872]{0:T(1024)(128)(2,1)} %dynamic-update-slice.4, bf16[589824]{0:T(1024)(128)(2,1)S(1)} %reshape.244, s32[]{} %constant.138) | dynamic-update-slice | bytes 2359300
  643.4 72.6 %dynamic-update-slice.7 = bf16[7087872]{0:T(1024)(128)(2,1)} dynamic-update-slice(bf16[7087872]{0:T(1024)(128)(2,1)} %dynamic-update-slice.6, bf16[2359296]{0:T(1024)(128)(2,1)} %bitcast.151, s32[]{} %constant.140) | dynamic-update-slice | bytes 9437188
  717.4 72.7 %dynamic-update-slice.9 = bf16[7087872]{0:T(1024)(128)(2,1)} dynamic-update-slice(bf16[7087872]{0:T(1024)(128)(2,1)} %dynamic-update-slice.8, bf16[2359296]{0:T(1024)(128)(2,1)} %reshape.246, s32[]{} %constant.142) | dynamic-update-slice | bytes 9437188
  797.8 16.0 %pad_bitcast_fusion = bf16[55392,128]{1,0:T(8,128)(2,1)} fusion(bf16[7087872]{0:T(1024)(128)(2,1)} %constant_dynamic-update-slice_fusion), kind=kLoop, calls=%fused_computation.8 | loop fusion | bytes 28356096 | tf_op jit(solution)/shard_map/convert_element_type | solution.py:228
  813.9 238.8 %reduce-scatter.12.cloned.1.call-done = bf16[13848,128]{1,0:T(8,128)(2,1)} async-done(((bf16[55392,128]{1,0:T(8,128)(2,1)}), bf16[13848,128]{1,0:T(8,128)(2,1)}) %reduce-scatter.12.cloned.1.call-update) | async-done | bytes 3545104
  1052.8 4.7 convert_element_type.211
  1057.4 75.5 %fusion = f32[1744,128]{1,0:T(8,128)S(1)} fusion(f32[13848,128]{1,0:T(8,128)} %convert_element_type.211), kind=kCustom, calls=%all-reduce-scatter | all-reduce-scatter fusion | flops 1785857 | bytes 7983616
  1137.8 36.7 %all-gather.12.cloned.1.call-done = bf16[8,1731,128]{2,1,0:T(8,128)(2,1)} async-done(((bf16[1,1731,128]{2,1,0:T(8,128)(2,1)}), bf16[8,1731,128]{2,1,0:T(8,128)(2,1)}) %all-gather.12.cloned.1.call-update) | async-done | bytes 3545104 | tf_op jit(solution)/shard_map/all_gather | solution.py:231
  1174.5 4.8 reshape.254
  1179.4 4.9 add_convert_fusion.1
  1184.4 239.5 %all-gather.10.cloned.1.call-done = bf16[55392,128]{1,0:T(8,128)(2,1)} async-done(((bf16[13848,128]{1,0:T(8,128)(2,1)}), bf16[55392,128]{1,0:T(8,128)(2,1)}) %all-gather.10.cloned.1.call-update) | async-done | bytes 14180368 | tf_op jit(solution)/shard_map/all_gather | solution.py:232
  1423.9 16.7 %convert_element_type.213 = f32[55392,128]{1,0:T(8,128)} convert(bf16[55392,128]{1,0:T(8,128)(2,1)} %all-gather.10.cloned.1.call-done) | non-fusion elementwise | flops 7090176 | bytes 42541056 | tf_op jit(solution)/shard_map/convert_element_type | solution.py:232
  1440.6 2.1 slice_bitcast_fusion
  1444.1 3.1 fusion.79
  1447.2 3.4 reshape.250
  1450.6 3.4 reshape.249
  1453.9 3.4 reshape.248
  1458.9 10.1 fusion.78
  1469.0 11.3 reshape.252
  1480.3 11.0 reshape.251
  (214 shorter events, 46.7 us)
Async XLA Ops:
  7.2 250.6 %copy-start = (bf16[768,768]{1,0:T(8,128)(2,1)S(1)}, bf16[768,768]{1,0:T(8,128)(2,1)}, u32[]{:S(2)}) copy-start(bf16[768,768]{1,0:T(8,128)(2,1)} %param.27) | copy-start | bytes 3538948
  7.2 5.9 copy-start.4
  7.2 120.3 %all-gather.8.cloned.1.call-start = ((), (), s32[]{:S(2)}) async-start(), calls=%async_computation.4 | async-start | bytes 7372800 | tf_op jit(solution)/shard_map/all_gather | solution.py:97
  7.3 5.8 copy-start.68
  8.1 20.4 %copy-start.31 = (f32[768]{0:T(1024)}, f32[768]{0:T(1024)S(1)}, u32[]{:S(2)}) copy-start(f32[768]{0:T(1024)S(1)} %convert_element_type.166) | copy-start | bytes 9220
  8.8 19.7 %copy-start.51 = (f32[768]{0:T(1024)}, f32[768]{0:T(1024)S(1)}, u32[]{:S(2)}) copy-start(f32[768]{0:T(1024)S(1)} %convert_element_type.167) | copy-start | bytes 9220
  10.5 18.0 %copy-start.23 = (f32[12,80]{1,0:T(8,128)}, f32[12,80]{1,0:T(8,128)S(1)}, u32[]{:S(2)}) copy-start(f32[12,80]{1,0:T(8,128)S(1)} %broadcast_multiply_fusion.1) | copy-start | bytes 11524
  13.1 15.4 %copy-start.27 = (f32[12,80]{1,0:T(8,128)}, f32[12,80]{1,0:T(8,128)S(1)}, u32[]{:S(2)}) copy-start(f32[12,80]{1,0:T(8,128)S(1)} %fusion.61) | copy-start | bytes 11524
  15.8 221.0 %all-gather.6.cloned.1.call-start = ((), (), s32[]{:S(2)}) async-start(), calls=%async_computation.3 | async-start | bytes 7372800 | tf_op jit(solution)/shard_map/all_gather | solution.py:98
  15.9 4.3 copy-start.45
  15.9 4.3 copy-start.59
  15.9 4.4 copy-start.60
  15.9 4.4 copy-start.61
  15.9 4.4 copy-start.62
  16.0 4.4 copy-start.47
  20.0 466.4 %reduce-scatter.10.cloned.1.call-start = ((), (), s32[]{:S(2)}) async-start(), calls=%async_computation.6 | async-start | bytes 7372800 | tf_op jit(solution)/shard_map/reduce_scatter | solution.py:180
  20.3 307.4 %copy-start.39 = (f32[768]{0:T(1024)}, f32[768]{0:T(1024)S(1)}, u32[]{:S(2)}) copy-start(f32[768]{0:T(1024)S(1)} %convert_element_type.180) | copy-start | bytes 9220
  20.3 237.5 %copy-start.37 = (f32[768]{0:T(1024)}, f32[768]{0:T(1024)S(1)}, u32[]{:S(2)}) copy-start(f32[768]{0:T(1024)S(1)} %convert_element_type.179) | copy-start | bytes 9220
  20.3 243.1 %copy-start.53 = (f32[768]{0:T(1024)}, f32[768]{0:T(1024)S(1)}, u32[]{:S(2)}) copy-start(f32[768]{0:T(1024)S(1)} %convert_element_type.181) | copy-start | bytes 9220
  24.3 4.0 copy-start.69
  28.4 108.7 %copy-start.56 = (s32[80]{0:T(128)}, s32[80]{0:T(128)S(1)}, u32[]{:S(2)}) copy-start(s32[80]{0:T(128)S(1)} %iota_add_fusion) | copy-start | bytes 964
  28.4 108.7 %copy-start.49 = (s32[12]{0:T(128)}, s32[12]{0:T(128)S(1)}, u32[]{:S(2)}) copy-start(s32[12]{0:T(128)S(1)} %and_select_fusion) | copy-start | bytes 148
  29.2 107.8 %copy-start.35 = (f32[1,12,80]{2,0,1:T(1,128)}, f32[1,12,80]{2,0,1:T(1,128)S(1)}, u32[]{:S(2)}) copy-start(f32[1,12,80]{2,0,1:T(1,128)S(1)} %fusion.71) | copy-start | bytes 11524
  257.8 5.7 slice-start
  257.8 5.7 slice-start.1
  263.0 8.2 copy-start.9
  263.0 64.7 %copy-start.29 = (f32[12,80]{1,0:T(8,128)}, f32[12,80]{1,0:T(8,128)S(1)}, u32[]{:S(2)}) copy-start(f32[12,80]{1,0:T(8,128)S(1)} %broadcast_multiply_fusion) | copy-start | bytes 11524
  263.5 64.2 %copy-start.33 = (f32[12,80]{1,0:T(8,128)}, f32[12,80]{1,0:T(8,128)S(1)}, u32[]{:S(2)}) copy-start(f32[12,80]{1,0:T(8,128)S(1)} %fusion.62) | copy-start | bytes 11524
  271.2 28.3 %copy-start.12 = (f32[12,80,3072]{2,1,0:T(8,128)}, f32[12,80,3072]{2,1,0:T(8,128)S(1)}, u32[]{:S(2)}) copy-start(f32[12,80,3072]{2,1,0:T(8,128)S(1)} %get-tuple-element.57) | copy-start | bytes 35389444
  299.4 18.8 %copy-start.10 = (f32[12,80,768]{2,1,0:T(8,128)S(1)}, f32[12,80,768]{2,1,0:T(8,128)}, u32[]{:S(2)}) copy-start(f32[12,80,768]{2,1,0:T(8,128)} %copy-done.9) | copy-start | bytes 8847364
  355.7 209.9 %reduce-scatter.8.cloned.1.call-start = ((), (), s32[]{:S(2)}) async-start(), calls=%async_computation.5 | async-start | bytes 7372800 | tf_op jit(solution)/shard_map/reduce_scatter | solution.py:177
  373.4 12.5 copy-start.6
  385.9 5.7 copy-start.3
  401.0 10.9 copy-start.14
  411.9 10.1 copy-start.11
  411.9 10.1 copy-start.30
  411.9 10.1 copy-start.34
  411.9 10.1 copy-start.40
  411.9 10.1 copy-start.54
  432.2 620.6 %reduce-scatter.12.cloned.1.call-start = ((), (), s32[]{:S(2)}) async-start(), calls=%async_computation.9 | async-start | bytes 17725440
  433.8 4.1 copy-start.16
  441.5 12.0 copy-start.42
  441.5 12.0 copy-start.5
  441.5 12.0 copy-start.24
  441.5 12.0 copy-start.28
  441.5 12.0 copy-start.32
  441.6 12.0 copy-start.52
  458.8 7.5 copy-start.38
  458.8 7.5 copy-start.55
  466.3 14.4 copy-start.36
  466.3 14.4 copy-start.50
  466.3 14.4 copy-start.57
  573.3 3.4 copy-start.22
  600.8 41.2 %copy-start.44 = (bf16[768]{0:T(1024)(128)(2,1)S(1)}, bf16[768]{0:T(1024)(128)(2,1)}, u32[]{:S(2)}) copy-start(bf16[768]{0:T(1024)(128)(2,1)} %get-tuple-element.29) | copy-start | bytes 4612
  643.4 72.6 %copy-start.48 = (bf16[3072]{0:T(1024)(128)(2,1)S(1)}, bf16[3072]{0:T(1024)(128)(2,1)}, u32[]{:S(2)}) copy-start(bf16[3072]{0:T(1024)(128)(2,1)} %get-tuple-element.64) | copy-start | bytes 18436
  717.4 72.7 %copy-start.43 = (bf16[768]{0:T(1024)(128)(2,1)S(1)}, bf16[768]{0:T(1024)(128)(2,1)}, u32[]{:S(2)}) copy-start(bf16[768]{0:T(1024)(128)(2,1)} %get-tuple-element.53) | copy-start | bytes 4612
  717.4 76.9 %copy-start.65 = (bf16[768]{0:T(1024)(128)(2,1)S(1)}, bf16[768]{0:T(1024)(128)(2,1)}, u32[]{:S(2)}) copy-start(bf16[768]{0:T(1024)(128)(2,1)} %get-tuple-element.20) | copy-start | bytes 4612
  717.4 78.4 %copy-start.64 = (bf16[768]{0:T(1024)(128)(2,1)S(1)}, bf16[768]{0:T(1024)(128)(2,1)}, u32[]{:S(2)}) copy-start(bf16[768]{0:T(1024)(128)(2,1)} %get-tuple-element.24) | copy-start | bytes 4612
  813.9 360.7 %all-gather.12.cloned.1.call-start = ((), (), s32[]{:S(2)}) async-start(), calls=%async_computation.8 | async-start | bytes 3999744 | tf_op jit(solution)/shard_map/all_gather | solution.py:231
  1057.4 76.8 %copy-start.66 = (u32[32]{0:T(128)S(1)}, u32[32]{0:T(128)}, u32[]{:S(2)}) copy-start(u32[32]{0:T(128)} %constant.130) | copy-start | bytes 388
  1132.9 2.6 collective-permute-start
  1137.8 286.1 %all-gather.10.cloned.1.call-start = ((), (), s32[]{:S(2)}) async-start(), calls=%async_computation.7 | async-start | bytes 17725440 | tf_op jit(solution)/shard_map/all_gather | solution.py:232
  1423.9 20.2 %copy-start.2 = (bf16[55392,128]{1,0:T(8,128)(2,1)S(1)}, bf16[55392,128]{1,0:T(8,128)(2,1)}, u32[]{:S(2)}) copy-start(bf16[55392,128]{1,0:T(8,128)(2,1)} %all-gather.10.cloned.1.call-done) | copy-start | bytes 42541060
  1480.3 11.0 copy-start.1
  (16 other events, 30.9 us)
Sparse Core Ops, SparseCore 0:
  15.9 111.5 all-gather.7
  129.7 107.0 all-gather.5
  355.8 102.6 reduce-scatter.9
  460.7 104.8 reduce-scatter.7
  814.0 238.7 reduce-scatter.11
  1137.9 36.6 all-gather.11
  1179.5 244.3 all-gather.9
where the time goes:
time: 1530 us; the launch traced here: 1500 us
  waiting for transfers between devices  762 us (50%)
  local copies, waits for them, and re-layouts  371 us (24%)
  matrix products  182 us (12%)
  other arithmetic  89.2 us (6%)
  blocking collectives  75.5 us (5%)
  between operations  15.9 us (1%)
    all_gather x1, waiting for transfers between devices, on_device(): lax.all_gather(share.astype(jnp.bfloat16), 'seq', axis=0, tiled=True)  240 us
    unnamed x9, waiting for transfers between devices  239 us
    unnamed x166, local copies, waits for them, and re-layouts  237 us
    all_gather x1, waiting for transfers between devices, on_device(): lax.all_gather(keys_local, 'seq', axis=1, tiled=True)  98.2 us
    all_gather x1, waiting for transfers between devices, on_device(): lax.all_gather(values_local, 'seq', axis=1, tiled=True)  77.3 us
    unnamed x1, blocking collectives  75.5 us
    reduce_scatter x1, waiting for transfers between devices, on_device(): lax.psum_scatter(grad_keys_term.astype(jnp.bfloat16), 'seq', scatter_dime...  71.6 us
    dot_general x6, matrix products, back_project(): jnp.einsum('ico,no->icn', grad, weight, preferred_element_type=jnp.float32)  39.5 us
  transfers between devices with their start and end apart: 8, of which 6 were waited for; matrix products, arithmetic and copies ran while one was open for 12% of the time, Pallas kernels for 0%

commit v1 on v0

--- a/solution.py
+++ b/solution.py
@@ -47,6 +47,21 @@
         preferred_element_type=jnp.float32,
     ) * HEAD_DIM ** (-0.5)
     return jnp.where(key_valid[:, None, None, :] > 0, raw, -1e30)
+
+
+def to_images(field):
+    return lax.all_to_all(field, "seq", split_axis=0, concat_axis=1, tiled=True)
+
+
+def to_slots(field):
+    return lax.all_to_all(field, "seq", split_axis=1, concat_axis=0, tiled=True)
+
+
+def sum_devices(grad):
+    share = lax.psum_scatter(
+        grad.astype(jnp.bfloat16), ("dp", "seq"), scatter_dimension=0, tiled=True
+    )
+    return lax.all_gather(share, ("dp", "seq"), axis=0, tiled=True).astype(jnp.float32)
 
 
 def on_device(
@@ -70,14 +85,14 @@
     second_shift,
     router_weight,
 ):
+    tokens = to_images(tokens)
+    grad_out = to_images(grad_out)
     images, slots, width = tokens.shape
-    total_slots = slots * lax.axis_size("seq")
+    total_slots = slots
+    lengths = lax.dynamic_slice_in_dim(lengths, lax.axis_index("seq") * images, images)
     counts = (lengths + 1) // 2
-    own_slot = lax.axis_index("seq") * slots + jnp.arange(slots, dtype=jnp.int32)
-    valid = (own_slot[None, :] < counts[:, None]).astype(jnp.float32)
-    key_valid = (jnp.arange(total_slots, dtype=jnp.int32)[None, :] < counts[:, None]).astype(
-        jnp.float32
-    )
+    valid = (jnp.arange(slots, dtype=jnp.int32)[None, :] < counts[:, None]).astype(jnp.float32)
+    key_valid = valid
     router_float = router_weight.astype(jnp.float32)
     inputs = tokens.astype(jnp.float32)
     first_norm, first_pull = jax.vjp(
@@ -93,10 +108,7 @@
     values_local = (project(normed, value_weight) + value_bias.astype(jnp.float32)).astype(
         jnp.bfloat16
     )
-    keys_all, values_all = (
-        lax.all_gather(keys_local, "seq", axis=1, tiled=True),
-        lax.all_gather(values_local, "seq", axis=1, tiled=True),
-    )
+    keys_all, values_all = keys_local, values_local
     scores = scores_of(queries, keys_all, key_valid)
     top = jnp.max(scores, axis=-1, keepdims=True)
     expo = jnp.exp(scores - top)
@@ -137,10 +149,7 @@
     grad_output_bias = column_sum(grad_branch_one)
     grad_output_weight = outer_sum(context_low, grad_branch_one)
     grad_context = back_project(grad_branch_one, output_weight).astype(jnp.bfloat16)
-    keys_back, values_back = (
-        lax.all_gather(keys_local, "seq", axis=1, tiled=True),
-        lax.all_gather(values_local, "seq", axis=1, tiled=True),
-    )
+    keys_back, values_back = keys_local, values_local
     probs_again = jnp.exp(scores_of(queries, keys_back, key_valid) - log_total)
     grad_probs = jnp.einsum(
         "iqhe,ikhe->ihqk",
@@ -173,16 +182,8 @@
         split_heads(grad_context),
         preferred_element_type=jnp.float32,
     ).reshape(images, total_slots, width)
-    grad_keys_own, grad_values_own = (
-        lax.psum_scatter(
-            grad_keys_term.astype(jnp.bfloat16), "seq", scatter_dimension=1, tiled=True
-        ).astype(jnp.float32),
-        lax.psum_scatter(
-            grad_values_term.astype(jnp.bfloat16), "seq", scatter_dimension=1, tiled=True
-        ).astype(jnp.float32),
-    )
-    grad_keys_low = grad_keys_own.astype(jnp.bfloat16)
-    grad_values_low = grad_values_own.astype(jnp.bfloat16)
+    grad_keys_low = grad_keys_term.astype(jnp.bfloat16)
+    grad_values_low = grad_values_term.astype(jnp.bfloat16)
     grad_query_bias = column_sum(grad_queries)
     grad_value_bias = column_sum(grad_values_low)
     grad_query_weight = outer_sum(normed, grad_queries)
@@ -200,17 +201,20 @@
     )
     grad_inputs, grad_first_gain, grad_first_shift = first_pull(grad_normed)
     tokens_grad = (grad_inputs + grad_middle).astype(jnp.bfloat16)
-    pieces = [
-        grad_query_weight,
+    mixed = to_slots(mixed)
+    tokens_grad = to_slots(tokens_grad)
+    grad_down_weight = sum_devices(grad_down_weight)
+    grad_up_weight = sum_devices(grad_up_weight)
+    four = sum_devices(
+        jnp.concatenate(
+            [grad_query_weight, grad_key_weight, grad_value_weight, grad_output_weight]
+        )
+    ).reshape(4, width, width)
+    small = [
         grad_query_bias,
-        grad_key_weight,
-        grad_value_weight,
         grad_value_bias,
-        grad_output_weight,
         grad_output_bias,
-        grad_up_weight,
         grad_up_bias,
-        grad_down_weight,
         grad_down_bias,
         grad_first_gain,
         grad_first_shift,
@@ -218,45 +222,22 @@
         grad_second_shift,
         grad_router_weight,
     ]
-    flat = jnp.concatenate([piece.reshape(-1) for piece in pieces])
-    devices = lax.axis_size("dp") * lax.axis_size("seq")
-    block = devices * 128
-    padded_length = -(-flat.shape[0] // block) * block
-    leading = padded_length - flat.shape[0]
-    flat = jnp.pad(flat, (leading, 0)).reshape(padded_length // 128, 128)
-    share = lax.psum_scatter(
-        flat.astype(jnp.bfloat16), "seq", scatter_dimension=0, tiled=True
-    ).astype(jnp.float32)
-    share = lax.psum_scatter(share, "dp", scatter_dimension=0, tiled=True)
-    share = lax.all_gather(share.astype(jnp.bfloat16), "dp", axis=0, tiled=True).astype(share.dtype)
-    summed = lax.all_gather(share.astype(jnp.bfloat16), "seq", axis=0, tiled=True).astype(
-        share.dtype
-    )
-    summed = summed.reshape(-1)
-    results = []
-    offset = leading
-    for piece in pieces:
-        results.append(summed[offset : offset + piece.size].reshape(piece.shape))
-        offset = offset + piece.size
+    small = lax.psum(jnp.concatenate([piece.reshape(-1, width) for piece in small]), ("dp", "seq"))
+    ratio = up_bias.shape[0] // width
     return (
         mixed,
         tokens_grad,
-        results[0],
-        results[1],
-        results[2],
-        results[3],
-        results[4],
-        results[5],
-        results[6],
-        results[7],
-        results[8],
-        results[9],
-        results[10],
-        results[11],
-        results[12],
-        results[13],
-        results[14],
-        results[15],
+        four[0],
+        small[0],
+        four[1],
+        four[2],
+        small[1],
+        four[3],
+        small[2],
+        grad_up_weight,
+        small[3 : 3 + ratio].reshape(-1),
+        grad_down_weight,
+        *[small[3 + ratio + i] for i in range(6)],
     )
 
 

time: 1530 us -> 807 us (0.53); the launches traced: 1500 us -> 801 us
  waiting for transfers between devices: 762 us -> 401 us
  local copies, waits for them, and re-layouts: 371 us -> 45.9 us
  matrix products: 182 us -> 157 us
  starting transfers between devices: 1.79 us -> 20.3 us
    all_gather x4 -> x3, waiting for transfers between devices: 452 us -> 83.4 us  [sum_devices(): lax.all_gather(share, ('dp', 'seq'), axis=0, tiled=True).astype(jnp.float32)]
    unnamed x9 -> x6, waiting for transfers between devices: 239 us -> 0.1 us
    unnamed x166 -> x125, local copies, waits for them, and re-layouts: 237 us -> 6.63 us
    reduce_scatter x2 -> x3, waiting for transfers between devices: 71.7 us -> 236 us  [sum_devices(): lax.psum_scatter(grad.astype(jnp.bfloat16), ('dp', 'seq'), scatter_dimens...]
    all_to_all x0 -> x4, waiting for transfers between devices: none -> 80.9 us  [the longest x2 46.5 us: to_images(): return lax.all_to_all(field, 'seq', split_axis=0, concat_axis=1, tiled=True)]
    unnamed x1 -> x0, blocking collectives: 75.5 us -> none
    psum x0 -> x1, blocking collectives: none -> 74.1 us  [on_device(): lax.psum(jnp.concatenate([piece.reshape(-1, width) for piece in small]),...]
    reshape x11 -> x10, local copies, waits for them, and re-layouts: 56 us -> 0.8 us  [the longest x1 0.61 us: on_device(): small[3:3 + ratio].reshape(-1)]
  transfers between devices with their start and end apart: 8 -> 10, of which waited for: 6 -> 8; matrix products, arithmetic and copies ran while one was open for 12% -> 19% of each run, Pallas kernels for 0% -> 0%
where the time goes in v1:
time: 807 us; the launch traced here: 801 us
  waiting for transfers between devices  401 us (50%)
  matrix products  157 us (19%)
  other arithmetic  87.3 us (11%)
  blocking collectives  74.1 us (9%)
  local copies, waits for them, and re-layouts  45.9 us (6%)
  starting transfers between devices  20.3 us (3%)
  between operations  15.3 us (2%)
    reduce_scatter x3, waiting for transfers between devices, sum_devices(): lax.psum_scatter(grad.astype(jnp.bfloat16), ('dp', 'seq'), scatter_dimens...  236 us
    all_gather x3, waiting for transfers between devices, sum_devices(): lax.all_gather(share, ('dp', 'seq'), axis=0, tiled=True).astype(jnp.float32)  83.4 us
    psum x1, blocking collectives, on_device(): lax.psum(jnp.concatenate([piece.reshape(-1, width) for piece in small]),...  74.1 us
    all_to_all x2, waiting for transfers between devices, to_images(): return lax.all_to_all(field, 'seq', split_axis=0, concat_axis=1, tiled=True)  46.5 us
    dot_general x6, matrix products, project(): jnp.einsum('icn,no->ico', left, right, preferred_element_type=jnp.float32)  37.1 us
    dot_general x6, matrix products, back_project(): jnp.einsum('ico,no->icn', grad, weight, preferred_element_type=jnp.float32)  36.8 us
    all_to_all x2, waiting for transfers between devices, to_slots(): return lax.all_to_all(field, 'seq', split_axis=1, concat_axis=0, tiled=True)  34.4 us
    dot_general x6, matrix products, outer_sum(): jnp.einsum('icn,ico->no', left, right, preferred_element_type=jnp.float32)  29 us
  transfers between devices with their start and end apart: 10, of which 8 were waited for; matrix products, arithmetic and copies ran while one was open for 19% of the time, Pallas kernels for 0%

profile of v1, /device:TPU:0, one launch (start us, length us, event | category | flops | bytes accessed | tf_op | source)
XLA Modules:
  0.0 800.9 jit_solution(2934206289322686921)
XLA Ops:
  7.3 6.5 all-to-all-start
  14.2 34.5 %all-to-all-done = bf16[12,80,768]{2,1,0:T(8,128)(2,1)S(1)} async-done(((bf16[12,80,768]{2,1,0:T(8,128)(2,1)}), bf16[12,80,768]{2,1,0:T(8,128)(2,1)S(1)}, u32[]{:S(2)}, u32[]{:S(2)}) %all-to-all-start) | async-done | bytes 1474592 | tf_op jit(solution)/shard_map/all_to_all | solution.py:53
  48.6 4.3 all-to-all-start.2
  53.3 2.0 copy.81
  56.1 2.4 add_convert_fusion.6
  59.7 2.4 add_convert_fusion.4
  62.2 2.7 copy.83
  64.9 4.8 add_convert_fusion.5
  69.7 3.7 copy.82
  73.4 1.9 fusion.52
  75.3 12.1 %all-to-all-done.2 = bf16[12,80,768]{2,1,0:T(8,128)(2,1)} async-done(((bf16[12,80,768]{2,1,0:T(8,128)(2,1)}), bf16[12,80,768]{2,1,0:T(8,128)(2,1)}, u32[]{:S(2)}, u32[]{:S(2)}) %all-to-all-start.2) | async-done | bytes 1474592 | tf_op jit(solution)/shard_map/all_to_all | solution.py:53
  87.4 3.4 copy.89
  90.8 2.4 convolution_convert_fusion.1
  93.2 4.2 copy.84
  97.4 12.0 %fusion.51 = (f32[3,12,320]{2,1,0:T(8,128)S(1)}, f32[3,12,320,320]{2,3,1,0:T(8,128)}) fusion(bf16[3,320,12,64]{1,3,2,0:T(8,128)(2,1)S(1)} %bitcast.158, bf16[3,320,12,64]{1,3,2,0:T(8,128)(2,1)} %bitcast.160, pred[3,320]{1,0:T(4,128)(4,1)S(1)} %convert_compare_fusion), kind=kOutput, calls=%fused_computation.134 | convolution fusion | flops 482906880 | bytes 17741760 | tf_op jit(solution)/shard_map/iqhe,ikhe->ihqk/dot_general | solution.py:43
  109.4 9.4 %fusion = f32[3,12,320]{2,1,0:T(8,128)S(1)} fusion(f32[3,12,320,320]{2,3,1,0:T(8,128)} %get-tuple-element.49, f32[3,12,320]{2,1,0:T(8,128)S(1)} %get-tuple-element.48), kind=kLoop, calls=%fused_computation.7 | loop fusion | flops 7361280 | bytes 14837760 | tf_op jit(solution)/shard_map/reduce_sum | solution.py:115
  118.8 9.5 %fusion.24 = bf16[3,12,64,320]{3,2,1,0:T(8,128)(2,1)S(1)} fusion(bf16[3,320,12,64]{1,3,2,0:T(8,128)(2,1)S(1)} %bitcast.167, f32[3,12,320,320]{2,3,1,0:T(8,128)} %get-tuple-element.49, f32[3,12,320]{2,1,0:T(8,128)S(1)} %fusion, f32[3,12,320]{2,1,0:T(8,128)S(1)} %get-tuple-element.48), kind=kOutput, calls=%fused_computation.81 | convolution fusion | flops 483655680 | bytes 17786880 | tf_op jit(solution)/shard_map/ihqk,ikhe->iqhe/dot_general | solution.py:118
  128.4 4.2 multiply_add_fusion.1
  132.6 2.1 reduce_sum.189
  134.7 2.4 multiply_reduce_fusion.7
  137.4 10.4 %fusion.23 = (u8[320,3072]{1,0:T(8,128)(4,1)S(1)}, u8[320,3072]{1,0:T(8,128)(4,1)S(1)}, f32[3,320,3072]{2,1,0:T(8,128)S(1)}) fusion(f32[3072]{0:T(1024)S(1)} %convert_element_type.218, bf16[768,3072]{1,0:T(8,128)(2,1)} %param.29, f32[3,320,768]{2,1,0:T(8,128)S(1)} %copy-done.4, f32[768]{0:T(1024)S(1)} %convert_element_type.216, ...), kind=kOutput, calls=%fused_computation.76 | convolution fusion | flops 4572856320 | bytes 21456384 | tf_op jit(solution)/shard_map/icn,no->ico/dot_general | solution.py:23
  147.8 28.5 %multiply_convert_fusion.1 = (bf16[3,320,3072]{2,1,0:T(8,128)(2,1)}, f32[3,320,3072]{2,1,0:T(8,128)}) fusion(f32[3,320,3072]{2,1,0:T(8,128)S(1)} %get-tuple-element.52, f32[3072]{0:T(1024)S(1)} %convert_element_type.218, u8[320,3072]{1,0:T(8,128)(4,1)S(1)} %get-tuple-element.19, u8[320,3072]{1,0:T(8,128)(4,1)S(1)} %get-tuple-element.18), kind=kLoop, calls=%fused_computation.17 | loop fusion | flops 209387520 | bytes 31469568 | tf_op jit(solution)/shard_map/convert_element_type | solution.py:130
  176.3 16.3 %convert_reduce_fusion = (f32[3072]{0:T(1024)S(1)}, bf16[3,320,3072]{2,1,0:T(8,128)(2,1)}) fusion(f32[3,320,3072]{2,1,0:T(8,128)} %get-tuple-element.41, bf16[3072,768]{1,0:T(8,128)(2,1)} %param.31, f32[3,320,768]{2,1,0:T(8,128)} %bitcast.170, f32[3,320]{1,0:T(4,128)S(1)} %fusion.44, f32[3,320,3072]{2,1,0:T(8,128)} %copy-done.14, ...), kind=kOutput, calls=%fused_computation.15 | convolution fusion | flops 4581454848 | bytes 37187328 | tf_op jit(solution)/shard_map/ico,no->icn/dot_general | solution.py:27
  192.6 11.6 %fusion.47 = (f32[768]{0:T(1024)S(1)}, f32[3,320]{1,0:T(4,128)S(1)}, f32[3,320,768]{2,1,0:T(8,128)}) fusion(f32[768]{0:T(1024)S(1)} %convert_element_type.215, f32[3,320,768]{2,1,0:T(8,128)} %get-tuple-element.50, f32[3,320]{1,0:T(4,128)S(1)} %broadcast_multiply_fusion, bf16[3,320,3072]{2,1,0:T(8,128)(2,1)} %get-tuple-element.62, bf16[768,3072]{1,0:T(8,128)(2,1)} %param.29), kind=kOutput, calls=%fused_computation.131 | convolution fusion | flops 4533532672 | bytes 16528896 | tf_op jit(solution)/shard_map/ico,no->icn/dot_general | solution.py:27
  204.2 7.3 bitcast_convert_fusion
  211.8 4.1 multiply_reduce_fusion.1
  216.3 12.8 %convert_reduce_fusion.4 = (f32[768]{0:T(1024)S(1)}, bf16[3,320,768]{2,1,0:T(8,128)(2,1)S(1)}, f32[3,320,768]{2,1,0:T(8,128)}, bf16[3,320,768]{2,1,0:T(8,128)(2,1)}, f32[3,320]{1,0:T(4,128)S(1)}) fusion(f32[3,320]{1,0:T(4,128)S(1)} %fusion.44, f32[4,3,80,768]{3,2,0,1:T(8,128)S(1)} %copy-done.23, f32[3,320]{1,0:T(4,128)S(1)} %negate_multiply_fusion.2, ...), kind=kOutput, calls=%fused_computation.58 | convolution fusion | flops 4543117312 | bytes 28343808 | tf_op jit(solution)/shard_map/icn,no->ico/dot_general | solution.py:23
  229.1 1.2 copy-done.61
  230.3 2.5 convolution_convert_fusion
  232.8 3.2 copy.90
  236.0 4.4 bitcast_convert_fusion.2
  240.4 9.5 %convert_reduce_fusion.1 = (f32[12,64]{1,0:T(8,128)S(1)}, bf16[3,12,64,320]{3,2,1,0:T(8,128)(2,1)S(1)}) fusion(bf16[3,320,12,64]{1,3,2,0:T(8,128)(2,1)S(1)} %bitcast.162, f32[3,12,320,320]{2,3,1,0:T(8,128)} %get-tuple-element.49, f32[3,12,320]{2,1,0:T(8,128)S(1)} %log_add_fusion), kind=kOutput, calls=%fused_computation.45 | convolution fusion | flops 481443072 | bytes 17743872 | tf_op jit(solution)/shard_map/ihqk,iqhe->ikhe/dot_general | solution.py:179
  249.9 2.8 bitcast_convert_fusion.3
  252.8 9.8 %bitcast_convert_fusion.1 = bf16[768,3072]{1,0:T(8,128)(2,1)} fusion(bf16[3,320,3072]{2,1,0:T(8,128)(2,1)} %get-tuple-element.62, f32[3,320,768]{2,1,0:T(8,128)S(1)} %copy-done.6, f32[768]{0:T(1024)S(1)} %convert_element_type.216, f32[768]{0:T(1024)S(1)} %convert_element_type.215, f32[3,320]{1,0:T(4,128)S(1)} %fusion.45, ...), kind=kOutput, calls=%fused_computation.31 | convolution fusion | flops 4535894016 | bytes 13579776 | tf_op jit(solution)/shard_map/icn,ico->no/dot_general | solution.py:31
  262.7 16.3 %multiply_reduce_fusion = (f32[3,12,320]{2,1,0:T(8,128)S(1)}, f32[3,12,320,320]{2,3,1,0:T(8,128)}) fusion(f32[3,12,320,320]{2,3,1,0:T(8,128)} %get-tuple-element.49, f32[3,12,320]{2,1,0:T(8,128)S(1)} %log_add_fusion, bf16[3,320,12,64]{1,3,2,0:T(8,128)(2,1)S(1)} %bitcast.163, bf16[3,320,12,64]{1,3,2,0:T(8,128)(2,1)} %bitcast.166), kind=kOutput, calls=%fused_computation.1 | convolution fusion | flops 482906880 | bytes 32532480 | tf_op jit(solution)/shard_map/iqhe,ikhe->ihqk/dot_general | solution.py:154
  279.0 12.8 %multiply_convert_fusion = bf16[3,12,320,320]{2,3,1,0:T(8,128)(2,1)S(1)} fusion(f32[3,12,320,320]{2,3,1,0:T(8,128)} %get-tuple-element.55, f32[3,12,320,320]{2,3,1,0:T(8,128)} %get-tuple-element.49, f32[3,12,320]{2,1,0:T(8,128)S(1)} %get-tuple-element.54, f32[3,12,320]{2,1,0:T(8,128)S(1)} %log_add_fusion), kind=kLoop, calls=%fused_computation | loop fusion | flops 14745600 | bytes 36956160 | tf_op jit(solution)/shard_map/convert_element_type | solution.py:161
  291.8 1.9 convert_reduce_fusion.2
  293.7 1.2 copy-done.24
  294.9 2.8 bitcast_convert_fusion.5
  297.7 2.8 multiply_convert_fusion.2
  300.6 1.8 bitcast_convert_fusion.4
  303.2 2.4 pad_maximum_fusion
  305.7 12.0 %reduce-scatter.8.cloned.1.call-done = bf16[96,768]{1,0:T(8,128)(2,1)} async-done(((bf16[3072,768]{1,0:T(8,128)(2,1)}), bf16[96,768]{1,0:T(8,128)(2,1)}) %reduce-scatter.8.cloned.1.call-update) | async-done | bytes 147472 | tf_op jit(solution)/shard_map/reduce_scatter | solution.py:61
  317.8 112.4 %reduce-scatter.6.cloned.1.call-done = bf16[24,3072]{1,0:T(8,128)(2,1)} async-done(((bf16[768,3072]{1,0:T(8,128)(2,1)}), bf16[24,3072]{1,0:T(8,128)(2,1)}) %reduce-scatter.6.cloned.1.call-update) | async-done | bytes 147472 | tf_op jit(solution)/shard_map/reduce_scatter | solution.py:61
  430.2 112.1 %reduce-scatter.4.cloned.1.call-done = bf16[96,768]{1,0:T(8,128)(2,1)} async-done(((bf16[3072,768]{1,0:T(8,128)(2,1)}), bf16[96,768]{1,0:T(8,128)(2,1)}) %reduce-scatter.4.cloned.1.call-update) | async-done | bytes 147472 | tf_op jit(solution)/shard_map/reduce_scatter | solution.py:61
  542.4 3.9 copy.87
  546.3 4.6 all-to-all-start.1
  551.0 3.4 multiply_reduce_fusion.4
  554.7 1.8 fusion.31
  556.5 1.7 fusion.34
  559.2 2.9 fusion.48
  562.1 1.4 multiply_reduce_fusion.2
  565.1 2.5 copy.97
  567.6 34.3 %all-to-all-done.1 = bf16[3,320,768]{2,0,1:T(4,128)(2,1)} async-done(((bf16[3,320,768]{2,0,1:T(4,128)(2,1)}), bf16[3,320,768]{2,0,1:T(4,128)(2,1)}, u32[]{:S(2)}, u32[]{:S(2)}) %all-to-all-start.1) | async-done | bytes 1474592 | tf_op jit(solution)/shard_map/all_to_all | solution.py:57
  602.0 4.4 all-to-all-start.3
  606.5 1.7 convert_reduce_fusion.3
  608.8 74.1 %psum.7 = f32[13,768]{1,0:T(8,128)S(1)} all-reduce(f32[13,768]{1,0:T(8,128)S(1)} %concatenate.8), channel_id=1, replica_groups=mesh['dp'=8,'seq'=4] {'dp','seq'}, use_global_device_ids=true, to_apply=%region_23.24 | all-reduce | flops 9984 | bytes 79872 | tf_op jit(solution)/shard_map/psum | solution.py:225
  684.2 2.8 copy.88
  687.1 2.8 copy.98
  689.9 6.8 convert_element_type.254
  696.8 25.3 %all-gather.6.cloned.1.call-done = bf16[768,3072]{1,0:T(8,128)(2,1)} async-done(((bf16[24,3072]{1,0:T(8,128)(2,1)}), bf16[768,3072]{1,0:T(8,128)(2,1)}) %all-gather.6.cloned.1.call-update) | async-done | bytes 4718608 | tf_op jit(solution)/shard_map/all_gather | solution.py:64
  722.1 7.4 convert_element_type.252
  729.4 58.1 %all-gather.4.cloned.1.call-done = bf16[3072,768]{1,0:T(8,128)(2,1)} async-done(((bf16[96,768]{1,0:T(8,128)(2,1)}), bf16[3072,768]{1,0:T(8,128)(2,1)}) %all-gather.4.cloned.1.call-update) | async-done | bytes 4718608 | tf_op jit(solution)/shard_map/all_gather | solution.py:64
  787.5 6.3 fusion.50
  (181 shorter events, 9.4 us)
Async XLA Ops:
  7.2 121.1 %copy-start = (bf16[768,768]{1,0:T(8,128)(2,1)S(1)}, bf16[768,768]{1,0:T(8,128)(2,1)}, u32[]{:S(2)}) copy-start(bf16[768,768]{1,0:T(8,128)(2,1)} %param.27) | copy-start | bytes 3538948
  7.2 6.6 copy-start.43
  7.2 6.6 copy-start.48
  7.2 6.6 copy-start.49
  7.2 6.6 copy-start.50
  7.3 6.6 copy-start.51
  7.3 6.6 copy-start.52
  7.3 6.7 copy-start.53
  7.3 6.7 copy-start.54
  7.3 6.7 copy-start.55
  7.3 6.7 copy-start.45
  7.3 6.7 copy-start.60
  7.3 41.3 %all-to-all-start = ((bf16[12,80,768]{2,1,0:T(8,128)(2,1)}), bf16[12,80,768]{2,1,0:T(8,128)(2,1)S(1)}, u32[]{:S(2)}, u32[]{:S(2)}) async-start(bf16[12,80,768]{2,1,0:T(8,128)(2,1)} %param.19), calls=%async_computation | async-start | bytes 2949120 | tf_op jit(solution)/shard_map/all_to_all | solution.py:53
  13.8 42.3 %copy-start.33 = (f32[768]{0:T(1024)}, f32[768]{0:T(1024)S(1)}, u32[]{:S(2)}) copy-start(f32[768]{0:T(1024)S(1)} %convert_element_type.201) | copy-start | bytes 9220
  13.9 114.4 %copy-start.41 = (f32[768]{0:T(1024)}, f32[768]{0:T(1024)S(1)}, u32[]{:S(2)}) copy-start(f32[768]{0:T(1024)S(1)} %convert_element_type.214) | copy-start | bytes 9220
  14.1 61.1 %copy-start.46 = (s32[3]{0:T(128)}, s32[3]{0:T(128)S(1)}, u32[]{:S(2)}) copy-start(s32[3]{0:T(128)S(1)} %and_select_fusion) | copy-start | bytes 40
  48.6 38.8 %all-to-all-start.2 = ((bf16[12,80,768]{2,1,0:T(8,128)(2,1)}), bf16[12,80,768]{2,1,0:T(8,128)(2,1)}, u32[]{:S(2)}, u32[]{:S(2)}) async-start(bf16[12,80,768]{2,1,0:T(8,128)(2,1)} %param.21), calls=%async_computation.2 | async-start | bytes 2949120 | tf_op jit(solution)/shard_map/all_to_all | solution.py:53
  53.0 264.7 %reduce-scatter.8.cloned.1.call-start = ((), (), s32[]{:S(2)}) async-start(), calls=%async_computation.11 | async-start | bytes 4866048 | tf_op jit(solution)/shard_map/reduce_scatter | solution.py:61
  55.4 3.2 copy-start.31
  56.0 3.7 copy-start.58
  56.1 2.5 copy-start.37
  56.1 2.5 copy-start.35
  64.9 32.5 %copy-start.7 = (bf16[3,320,768]{1,2,0:T(8,128)(2,1)}, bf16[3,320,768]{1,2,0:T(8,128)(2,1)S(1)}, u32[]{:S(2)}) copy-start(bf16[3,320,768]{1,2,0:T(8,128)(2,1)S(1)} %copy.83) | copy-start | bytes 4423684
  75.2 18.0 %copy-start.39 = (f32[1,3,320]{2,0,1:T(1,128)}, f32[1,3,320]{2,0,1:T(1,128)S(1)}, u32[]{:S(2)}) copy-start(f32[1,3,320]{2,0,1:T(1,128)S(1)} %fusion.52) | copy-start | bytes 11524
  87.4 3.4 copy-start.11
  87.4 3.4 copy-start.56
  109.4 9.4 %copy-start.18 = (bf16[3,320,768]{1,2,0:T(8,128)(2,1)S(1)}, bf16[3,320,768]{1,2,0:T(8,128)(2,1)}, u32[]{:S(2)}) copy-start(bf16[3,320,768]{1,2,0:T(8,128)(2,1)} %copy.82) | copy-start | bytes 4423684
  118.8 9.6 %copy-start.2 = (f32[4,3,80,768]{3,2,0,1:T(8,128)S(1)}, f32[4,3,80,768]{3,2,0,1:T(8,128)}, u32[]{:S(2)}) copy-start(f32[4,3,80,768]{3,2,0,1:T(8,128)} %copy.81) | copy-start | bytes 8847364
  128.3 4.3 copy-start.26
  134.7 2.7 copy-start.4
  147.8 28.5 %copy-start.14 = (f32[3,320,3072]{2,1,0:T(8,128)}, f32[3,320,3072]{2,1,0:T(8,128)S(1)}, u32[]{:S(2)}) copy-start(f32[3,320,3072]{2,1,0:T(8,128)S(1)} %get-tuple-element.52) | copy-start | bytes 35389444
  192.6 11.6 %copy-start.19 = (bf16[3,320,3072]{2,1,0:T(8,128)(2,1)S(1)}, bf16[3,320,3072]{2,1,0:T(8,128)(2,1)}, u32[]{:S(2)}) copy-start(bf16[3,320,3072]{2,1,0:T(8,128)(2,1)} %get-tuple-element.40) | copy-start | bytes 17694724
  192.6 11.6 %copy-start.22 = (f32[4,3,80,768]{3,2,0,1:T(8,128)S(1)}, f32[4,3,80,768]{3,2,0,1:T(8,128)}, u32[]{:S(2)}) copy-start(f32[4,3,80,768]{3,2,0,1:T(8,128)} %copy.89) | copy-start | bytes 8847364
  211.5 218.7 %reduce-scatter.6.cloned.1.call-start = ((), (), s32[]{:S(2)}) async-start(), calls=%async_computation.9 | async-start | bytes 4866048 | tf_op jit(solution)/shard_map/reduce_scatter | solution.py:61
  211.8 4.2 copy-start.5
  211.8 4.5 copy-start.23
  240.4 9.5 %copy-start.12 = (bf16[3,320,768]{2,1,0:T(8,128)(2,1)S(1)}, bf16[3,320,768]{2,1,0:T(8,128)(2,1)}, u32[]{:S(2)}) copy-start(bf16[3,320,768]{2,1,0:T(8,128)(2,1)} %copy-done.10) | copy-start | bytes 4423684
  249.9 2.9 copy-start.16
  249.9 2.9 copy-start.6
  262.6 279.7 %reduce-scatter.4.cloned.1.call-start = ((), (), s32[]{:S(2)}) async-start(), calls=%async_computation.7 | async-start | bytes 4866048 | tf_op jit(solution)/shard_map/reduce_scatter | solution.py:61
  279.0 12.8 %copy-start.9 = (bf16[3,320,768]{1,2,0:T(8,128)(2,1)S(1)}, bf16[3,320,768]{1,2,0:T(8,128)(2,1)}, u32[]{:S(2)}) copy-start(bf16[3,320,768]{1,2,0:T(8,128)(2,1)} %copy.84) | copy-start | bytes 4423684
  291.8 3.1 copy-start.13
  294.9 2.8 copy-start.8
  300.6 1.9 copy-start.28
  300.6 2.3 copy-start.29
  300.6 2.6 copy-start.30
  305.6 236.7 %copy-start.44 = (bf16[768]{0:T(1024)(128)(2,1)S(1)}, bf16[768]{0:T(1024)(128)(2,1)}, u32[]{:S(2)}) copy-start(bf16[768]{0:T(1024)(128)(2,1)} %param.37) | copy-start | bytes 4612
  305.6 384.3 %all-gather.8.cloned.1.call-start = ((), (), s32[]{:S(2)}) async-start(), calls=%async_computation.12 | async-start | bytes 4866048 | tf_op jit(solution)/shard_map/all_gather | solution.py:64
  317.7 404.3 %all-gather.6.cloned.1.call-start = ((), (), s32[]{:S(2)}) async-start(), calls=%async_computation.10 | async-start | bytes 4866048 | tf_op jit(solution)/shard_map/all_gather | solution.py:64
  430.2 357.3 %all-gather.4.cloned.1.call-start = ((), (), s32[]{:S(2)}) async-start(), calls=%async_computation.8 | async-start | bytes 4866048 | tf_op jit(solution)/shard_map/all_gather | solution.py:64
  542.4 8.6 %copy-start.42 = (f32[768]{0:T(1024)S(1)}, f32[768]{0:T(1024)}, u32[]{:S(2)}) copy-start(f32[768]{0:T(1024)} %copy-done.41) | copy-start | bytes 9220
  546.3 55.7 %all-to-all-start.1 = ((bf16[3,320,768]{2,0,1:T(4,128)(2,1)}), bf16[3,320,768]{2,0,1:T(4,128)(2,1)}, u32[]{:S(2)}, u32[]{:S(2)}) async-start(bf16[3,320,768]{2,0,1:T(4,128)(2,1)} %copy.87), calls=%async_computation.1 | async-start | bytes 3932160 | tf_op jit(solution)/shard_map/all_to_all | solution.py:57
  550.9 3.4 copy-start.40
  550.9 3.4 copy-start.47
  550.9 3.5 copy-start.21
  551.0 3.7 copy-start.57
  556.5 2.4 copy-start.17
  556.5 2.7 copy-start.27
  556.5 2.7 copy-start.32
  556.5 2.7 copy-start.34
  559.2 2.9 copy-start.38
  559.2 3.0 copy-start.36
  602.0 85.1 %all-to-all-start.3 = ((bf16[3,320,768]{2,0,1:T(4,128)(2,1)}), bf16[3,320,768]{2,0,1:T(4,128)(2,1)}, u32[]{:S(2)}, u32[]{:S(2)}) async-start(bf16[3,320,768]{2,0,1:T(4,128)(2,1)} %copy.97), calls=%async_computation.3 | async-start | bytes 3932160 | tf_op jit(solution)/shard_map/all_to_all | solution.py:57
  787.5 6.3 copy-start.1
  (8 other events, 12.6 us)
Sparse Core Ops, SparseCore 0:
  211.6 106.0 reduce-scatter.7
  324.1 106.0 reduce-scatter.5
  436.2 106.0 reduce-scatter.3
  545.3 94.9 all-gather.7
  643.4 78.6 all-gather.5
  725.1 62.3 all-gather.3

commit v2 on v1

v2 whole, which is shorter than its diff:
```python
import functools
import math

import jax
import jax.numpy as jnp
from jax import lax
from jax.experimental import pallas as pl
from jax.experimental.pallas import tpu as pltpu
from jax.sharding import PartitionSpec as P

HEADS = 12
HEAD_DIM = 64
EPSILON = 1e-06
PAIR = 2 * HEAD_DIM
LANES = 128
SCALE = HEAD_DIM ** (-0.5)
SCORE_FACTOR = SCALE * math.log2(math.e)
ROOT_HALF = math.sqrt(0.5)
DENSITY = 1.0 / math.sqrt(2.0 * math.pi)
MASKED = -1e30
TILE = 256
VMEM = 56 * 1024 * 1024
F32 = jnp.float32
BF16 = jnp.bfloat16

QB, VB, OB, G1, S1, G2, S2, RW, DB = range(9)


def nn(a, b):
    return lax.dot_general(a, b, (((1,), (0,)), ((), ())), preferred_element_type=F32)


def nt(a, b):
    return lax.dot_general(a, b, (((1,), (1,)), ((), ())), preferred_element_type=F32)


def tn(a, b):
    return lax.dot_general(a, b, (((0,), (0,)), ((), ())), preferred_element_type=F32)


def hat(field):
    mean = jnp.mean(field, axis=-1, keepdims=True)
    centred = field - mean
    spread = jnp.mean(centred * centred, axis=-1, keepdims=True)
    scale = lax.rsqrt(spread + EPSILON)
    return centred * scale, scale


def hat_back(grad, normal, scale):
    first = jnp.mean(grad, axis=-1, keepdims=True)
    second = jnp.mean(grad * normal, axis=-1, keepdims=True)
    return scale * (grad - first - normal * second)


def row_sum(field):
    return jnp.sum(field, axis=0, keepdims=True)


def head_masks():
    lane = lax.broadcasted_iota(jnp.int32, (1, PAIR), 1)
    return [
        jnp.where(lane < HEAD_DIM, 1.0, 0.0).astype(BF16),
        jnp.where(lane < HEAD_DIM, 0.0, 1.0).astype(BF16),
    ]


def attention_kernel(
    counts,
    x_ref,
    vec,
    wq,
    wk,
    wv,
    wo,
    normed_ref,
    q_ref,
    k_ref,
    v_ref,
    ctx_ref,
    middle_ref,
    one_ref,
    second_ref,
    gate_ref,
    row_ref,
    lse_ref,
):
    slots = x_ref.shape[1]
    count = counts[pl.program_id(0)]
    x = x_ref[0].astype(F32)
    normal, _ = hat(x)
    normed = (normal * vec[G1 : G1 + 1] + vec[S1 : S1 + 1]).astype(BF16)
    normed_ref[0] = normed
    logit = jnp.sum(normed.astype(F32) * vec[RW : RW + 1], axis=-1, keepdims=True)
    gate = jax.nn.sigmoid(logit)
    inside = lax.broadcasted_iota(jnp.int32, (slots, 1), 0) < count
    row = jnp.where(inside, gate, 0.0)
    gate_ref[0] = jnp.broadcast_to(gate, (slots, LANES))
    row_ref[0] = jnp.broadcast_to(row, (slots, LANES))
    q_ref[0] = (nn(normed, wq[...]) + vec[QB : QB + 1]).astype(BF16)
    k_ref[0] = nn(normed, wk[...]).astype(BF16)
    v_ref[0] = (nn(normed, wv[...]) + vec[VB : VB + 1]).astype(BF16)
    key_mask = jnp.where(
        lax.broadcasted_iota(jnp.int32, (1, slots), 1) < count, 0.0, MASKED
    )
    masks = head_masks()
    lane = lax.broadcasted_iota(jnp.int32, (1, LANES), 1)
    ones = jnp.ones((slots, LANES), BF16)
    lse = jnp.zeros((slots, LANES), F32)
    for pair in range(HEADS // 2):
        at = slice(pair * PAIR, (pair + 1) * PAIR)
        queries = q_ref[0, :, at]
        keys = k_ref[0, :, at]
        values = jnp.concatenate([v_ref[0, :, at], ones], axis=1)
        halves = []
        for e in range(2):
            scores = nt(queries * masks[e], keys) * SCORE_FACTOR + key_mask
            top = jnp.max(scores, axis=-1, keepdims=True)
            expo = jnp.exp2(scores - top).astype(BF16)
            mixed = nn(expo, values)
            total = mixed[:, PAIR:]
            halves.append(mixed[:, :PAIR] / total)
            lse = jnp.where(lane == 2 * pair + e, top + jnp.log2(total), lse)
        low = jnp.where(lane < HEAD_DIM, halves[0], halves[1])
        ctx_ref[0, :, at] = low.astype(BF16)
    lse_ref[0] = lse
    one = nn(ctx_ref[0], wo[...]) + vec[OB : OB + 1]
    one_ref[0] = one
    middle = x + row * one
    middle_ref[0] = middle
    again, _ = hat(middle)
    second_ref[0] = (again * vec[G2 : G2 + 1] + vec[S2 : S2 + 1]).astype(BF16)


def run_attention(counts, tokens, vectors, wq, wk, wv, wo):
    images, slots, width = tokens.shape
    image = lambda *shape: pl.BlockSpec((1, slots) + shape, lambda i, c: (i, 0, 0))
    whole = lambda a: pl.BlockSpec(a.shape, lambda i, c: (0,) * a.ndim)
    like = lambda lanes, dtype: jax.ShapeDtypeStruct((images, slots, lanes), dtype)
    outs = [(width, BF16)] * 5 + [(width, F32)] * 2 + [(width, BF16)] + [(LANES, F32)] * 3
    flops = 2 * images * slots * width * (4 * width + 2 * slots)
    return pl.pallas_call(
        attention_kernel,
        grid_spec=pltpu.PrefetchScalarGridSpec(
            num_scalar_prefetch=1,
            grid=(images,),
            in_specs=[image(width)] + [whole(a) for a in (vectors, wq, wk, wv, wo)],
            out_specs=[image(lanes) for lanes, _ in outs],
        ),
        out_shape=[like(*o) for o in outs],
        compiler_params=pltpu.CompilerParams(vmem_limit_bytes=VMEM),
        cost_estimate=pl.CostEstimate(
            flops=flops, bytes_accessed=40_000_000, transcendentals=images * HEADS * slots * slots
        ),
        name="attention_forward",
    )(counts, tokens, vectors, wq, wk, wv, wo)


def feed_body(second, back, up, bias, down, two, pulled, down_grad, up_grad, bias_grad):
    hidden = nn(second[...], up[...]) + bias[...]
    phi = 0.5 + 0.5 * lax.erf(hidden * ROOT_HALF)
    density = DENSITY * jnp.exp(-0.5 * hidden * hidden)
    active = (hidden * phi).astype(BF16)
    slope = phi + hidden * density
    two[...] += nn(active, down[...])
    grad_hidden = nt(back[...], down[...]) * slope
    low = grad_hidden.astype(BF16)
    bias_grad[...] = row_sum(low.astype(F32))
    pulled[...] += nt(low, up[...])
    down_grad[...] = tn(active, back[...]).astype(BF16)
    up_grad[...] = tn(second[...], low).astype(BF16)


def feed_first_kernel(
    half,
    second,
    grad_out,
    row,
    up,
    bias,
    down,
    back,
    two,
    pulled,
    down_grad,
    up_grad,
    bias_grad,
    back_sum,
):
    @pl.when(pl.program_id(0) == 0)
    def _():
        value = (row[:, :1] * grad_out[...].astype(F32)).astype(BF16)
        back[...] = value
        back_sum[...] = row_sum(value.astype(F32))
        two[...] = jnp.zeros_like(two)
        pulled[...] = jnp.zeros_like(pulled)

    feed_body(second, back, up, bias, down, two, pulled, down_grad, up_grad, bias_grad)


def feed_second_kernel(
    half,
    second,
    grad_out,
    row,
    up,
    bias,
    down,
    back,
    two_in,
    pulled_in,
    middle,
    one,
    gate,
    vec,
    down_grad,
    up_grad,
    bias_grad,
    mixed,
    grad_middle,
    grad_one,
    grad_logit,
    sums,
    two,
    pulled,
    *,
    block,
):
    @pl.when(pl.program_id(0) == 0)
    def _():
        two[...] = two_in[...]
        pulled[...] = pulled_in[...]

    feed_body(second, back, up, bias, down, two, pulled, down_grad, up_grad, bias_grad)

    @pl.when(pl.program_id(0) == pl.num_programs(0) - 1)
    def _():
        width = second.shape[1]
        zero = jnp.zeros((1, width), F32)

        def step(b, carry):
            gain_sum, shift_sum, one_sum = carry
            at = pl.ds(pl.multiple_of(b * block, block), block)
            upstream = grad_out[at, :].astype(F32)
            weight = row[at, :1]
            branch_two = two[at, :] + vec[DB : DB + 1]
            centre = middle[at, :]
            mixed[at, :] = (centre + weight * branch_two).astype(BF16)
            normal, scale = hat(centre)
            grad = pulled[at, :]
            gain_sum = gain_sum + row_sum(grad * normal)
            shift_sum = shift_sum + row_sum(grad)
            total = hat_back(grad * vec[G2 : G2 + 1], normal, scale) + upstream
            grad_middle[at, :] = total
            low = (weight * total).astype(BF16)
            grad_one[at, :] = low
            one_sum = one_sum + row_sum(low.astype(F32))
            gated = jnp.sum(upstream * branch_two + total * one[at, :], axis=-1, keepdims=True)
            grad_logit[at, :] = weight * (1.0 - gate[at, :]) * gated
            return gain_sum, shift_sum, one_sum

        gain_sum, shift_sum, one_sum = lax.fori_loop(
            0, second.shape[0] // block, step, (zero, zero, zero)
        )
        sums[0:1] = gain_sum
        sums[1:2] = shift_sum
        sums[2:3] = one_sum


def run_feed(which, second, grad_out, row, up, bias, down, later=None):
    rows, width = second.shape
    units = up.shape[1] // 2
    tiles = units // TILE
    whole = lambda a: pl.BlockSpec(a.shape, lambda t, h: (0,) * len(a.shape))
    shape = jax.ShapeDtypeStruct
    wide, tall = (
        pl.BlockSpec((width, TILE), lambda t, h: (0, h[0] * tiles + t)),
        pl.BlockSpec((TILE, width), lambda t, h: (h[0] * tiles + t, 0)),
    )
    in_specs = [whole(second), whole(grad_out), whole(row)]
    in_specs += [wide, pl.BlockSpec((1, TILE), lambda t, h: (0, h[0] * tiles + t)), tall]
    tile_outs = [shape((units, width), BF16), shape((width, units), BF16), shape((1, units), F32)]
    tile_specs = [
        pl.BlockSpec((TILE, width), lambda t, h: (t, 0)),
        pl.BlockSpec((width, TILE), lambda t, h: (0, t)),
        pl.BlockSpec((1, TILE), lambda t, h: (0, t)),
    ]
    field = lambda dtype: shape((rows, width), dtype)
    args = [second, grad_out, row, up, bias, down]
    scratch = []
    if later is None:
        body = feed_first_kernel
        outs = [field(BF16), field(F32), field(F32)] + tile_outs + [shape((1, width), F32)]
        specs = [whole(o) for o in outs[:3]] + tile_specs + [whole(outs[-1])]
    else:
        body = functools.partial(feed_second_kernel, block=math.gcd(rows, 80))
        args += later
        in_specs += [whole(a) for a in later]
        more = [field(BF16), field(F32), field(BF16), shape(row.shape, F32), shape((8, width), F32)]
        outs = tile_outs + more
        specs = tile_specs + [whole(o) for o in more]
        scratch = [pltpu.VMEM((rows, width), F32)] * 2
    return pl.pallas_call(
        body,
        grid_spec=pltpu.PrefetchScalarGridSpec(
            num_scalar_prefetch=1,
            grid=(tiles,),
            in_specs=in_specs,
            out_specs=specs,
            scratch_shapes=scratch,
        ),
        out_shape=outs,
        compiler_params=pltpu.CompilerParams(vmem_limit_bytes=VMEM),
        cost_estimate=pl.CostEstimate(
            flops=12 * rows * width * units, bytes_accessed=30_000_000, transcendentals=2 * rows * units
        ),
        name="feed_first" if later is None else "feed_second",
    )(which, *args)


def attention_back_kernel(
    counts,
    x_ref,
    q_ref,
    k_ref,
    v_ref,
    lse_ref,
    grad_one,
    grad_middle,
    grad_logit,
    normed,
    vec,
    wq,
    wk,
    wv,
    wo,
    *rest,
    image,
):
    grads, tokens_grad, sums, pulled = rest[-4:]
    slots = x_ref.shape[1]
    count = counts[image]
    pulled[...] = nt(grad_one[0], wo[...]).astype(BF16)
    lse = lse_ref[0].T
    inside = lax.broadcasted_iota(jnp.int32, (slots, 1), 0) < count
    masks = head_masks()
    for pair in range(HEADS // 2):
        at = slice(pair * PAIR, (pair + 1) * PAIR)
        queries, keys, values = q_ref[0, :, at], k_ref[0, :, at], v_ref[0, :, at]
        above = pulled[:, at]
        grad_q = grad_k = grad_v = None
        for e in range(2):
            h = 2 * pair + e
            own_keys = keys * masks[e]
            scores = nt(own_keys, queries) * SCORE_FACTOR - lse[h : h + 1]
            probs = jnp.exp2(jnp.where(inside, scores, MASKED))
            slope = probs * nt(values * masks[e], above)
            centre = row_sum(slope)
            low = (slope - probs * centre).astype(BF16)
            terms = (
                tn(low, own_keys),
                nn(low, queries * masks[e]),
                nn(probs.astype(BF16), above * masks[e]),
            )
            if e == 0:
                grad_q, grad_k, grad_v = terms
            else:
                grad_q, grad_k, grad_v = (
                    grad_q + terms[0],
                    grad_k + terms[1],
                    grad_v + terms[2],
                )
        grads[0, 0, :, at] = (grad_q * SCALE).astype(BF16)
        grads[1, 0, :, at] = (grad_k * SCALE).astype(BF16)
        grads[2, 0, :, at] = grad_v.astype(BF16)
    logit = grad_logit[0, :, :1]
    total = (
        nt(grads[0, 0], wq[...])
        + nt(grads[1, 0], wk[...])
        + nt(grads[2, 0], wv[...])
        + logit * vec[RW : RW + 1]
    )
    normal, scale = hat(x_ref[0].astype(F32))
    sums[0:1] = row_sum(grads[0, 0].astype(F32))
    sums[1:2] = row_sum(grads[2, 0].astype(F32))
    sums[2:3] = row_sum(total * normal)
    sums[3:4] = row_sum(total)
    sums[4:5] = row_sum(normed[0].astype(F32) * logit)
    back = hat_back(total * vec[G1 : G1 + 1], normal, scale)
    tokens_grad[0] = (back + grad_middle[0]).astype(BF16)


def run_attention_back(image, fields, vectors, weights, counts, before):
    images, slots, width = fields[0].shape
    at = lambda a: pl.BlockSpec((1,) + a.shape[1:], lambda i, c: (image, 0, 0))
    whole = lambda a: pl.BlockSpec(a.shape, lambda i, c: (0,) * a.ndim)
    args = [*fields, vectors, *weights]
    in_specs = [at(a) for a in fields] + [whole(a) for a in (vectors, *weights)]
    aliases = {}
    if before is not None:
        for n, array in enumerate(before):
            aliases[1 + len(args)] = n
            args.append(array)
            in_specs.append(pl.BlockSpec(memory_space=pl.ANY))
    shape = jax.ShapeDtypeStruct
    return pl.pallas_call(
        functools.partial(attention_back_kernel, image=image),
        grid_spec=pltpu.PrefetchScalarGridSpec(
            num_scalar_prefetch=1,
            grid=(1,),
            in_specs=in_specs,
            out_specs=[
                pl.BlockSpec((3, 1, slots, width), lambda i, c: (0, image, 0, 0)),
                pl.BlockSpec((1, slots, width), lambda i, c: (image, 0, 0)),
                pl.BlockSpec((8, width), lambda i, c: (0, 0)),
            ],
            scratch_shapes=[pltpu.VMEM((slots, width), BF16)],
        ),
        out_shape=[
            shape((3, images, slots, width), BF16),
            shape((images, slots, width), BF16),
            shape((8, width), F32),
        ],
        input_output_aliases=aliases,
        compiler_params=pltpu.CompilerParams(vmem_limit_bytes=VMEM),
        cost_estimate=pl.CostEstimate(
            flops=2 * slots * width * (4 * width + 5 * slots),
            bytes_accessed=12_000_000,
            transcendentals=HEADS * slots * slots,
        ),
        name="attention_backward",
    )(counts, *args)


def outer_kernel(half, normed, ctx, grads, grad_one, out):
    which = lax.rem(pl.program_id(0) + 2 * half[0], 4)

    @pl.when(which < 3)
    def _():
        out[0] = tn(normed[...], grads[0]).astype(BF16)

    @pl.when(which == 3)
    def _():
        out[0] = tn(ctx[...], grad_one[...]).astype(BF16)


def run_outer(half, normed, ctx, grads, grad_one):
    rows, width = normed.shape
    whole = lambda a: pl.BlockSpec(a.shape, lambda s, h: (0,) * a.ndim)
    return pl.pallas_call(
        outer_kernel,
        grid_spec=pltpu.PrefetchScalarGridSpec(
            num_scalar_prefetch=1,
            grid=(4,),
            in_specs=[
                whole(normed),
                whole(ctx),
                pl.BlockSpec(
                    (1, rows, width),
                    lambda s, h: (jnp.minimum(lax.rem(s + 2 * h[0], 4), 2), 0, 0),
                ),
                whole(grad_one),
            ],
            out_specs=pl.BlockSpec((1, width, width), lambda s, h: (s, 0, 0)),
        ),
        out_shape=jax.ShapeDtypeStruct((4, width, width), BF16),
        compiler_params=pltpu.CompilerParams(vmem_limit_bytes=VMEM),
        cost_estimate=pl.CostEstimate(
            flops=8 * rows * width * width, bytes_accessed=15_000_000, transcendentals=0
        ),
        name="outer",
    )(half, normed, ctx, grads, grad_one)


def bits_of(axis):
    size = lax.axis_size(axis)
    count = size.bit_length() - 1
    if size != 1 << count:
        raise ValueError("axis size")
    return [(axis, b) for b in range(count)]


def bit_of(step):
    axis, b = step
    return (lax.axis_index(axis) >> b) & 1


def swap(field, step):
    axis, b = step
    return lax.ppermute(field, axis, [(i, i ^ (1 << b)) for i in range(lax.axis_size(axis))])


def add_low(a, b):
    return (a.astype(F32) + b.astype(F32)).astype(BF16)


def halves(field, step):
    half = field.shape[0] // 2
    own = bit_of(step)
    return (
        lax.dynamic_slice_in_dim(field, (1 - own) * half, half),
        lax.dynamic_slice_in_dim(field, own * half, half),
    )


def scatter_sum(field, order):
    for step in order:
        if field.shape[0] % 2:
            field = add_low(field, swap(field, step))
            continue
        send, keep = halves(field, step)
        field = add_low(keep, swap(send, step))
    return field


def ordered(own, other, step, axis=0):
    return jnp.where(
        bit_of(step) == 0,
        jnp.concatenate([own, other], axis=axis),
        jnp.concatenate([other, own], axis=axis),
    )


def gather(field, order, rows):
    scattered = []
    for step in order:
        scattered.append(rows % 2 == 0)
        if rows % 2 == 0:
            rows //= 2
    for step, was in zip(reversed(order), reversed(scattered)):
        if was:
            field = ordered(field, swap(field, step), step)
    return field


def sum_over(field, order):
    return gather(scatter_sum(field, order), order, field.shape[0])


def to_images(field):
    return lax.all_to_all(field, "seq", split_axis=0, concat_axis=1, tiled=True)


def to_slots(field):
    return lax.all_to_all(field, "seq", split_axis=1, concat_axis=0, tiled=True)


def on_device(
    tokens,
    lengths,
    grad_out,
    query_weight,
    query_bias,
    key_weight,
    value_weight,
    value_bias,
    output_weight,
    output_bias,
    up_weight,
    up_bias,
    down_weight,
    down_bias,
    first_gain,
    first_shift,
    second_gain,
    second_shift,
    router_weight,
):
    tokens = to_images(tokens)
    grad_out = to_images(grad_out)
    images, slots, width = tokens.shape
    rows = images * slots
    lengths = lax.dynamic_slice_in_dim(lengths, lax.axis_index("seq") * images, images)
    counts = (lengths + 1) // 2
    vectors = [
        query_bias,
        value_bias,
        output_bias,
        first_gain,
        first_shift,
        second_gain,
        second_shift,
        router_weight,
        down_bias,
    ]
    vectors = jnp.pad(jnp.stack(vectors).astype(F32), ((0, 16 - len(vectors)), (0, 0)))
    flat = lambda field: field.reshape(rows, field.shape[-1])
    cube = lambda field: field.reshape(images, slots, field.shape[-1])

    weights = (query_weight, key_weight, value_weight, output_weight)
    normed, queries, keys, values, context, middle, one, second, gate, row, lse = run_attention(
        counts, tokens, vectors, *weights
    )

    first, *others = bits_of("dp")
    own = bit_of(first)
    mine, theirs = own.reshape(1), (1 - own).reshape(1)
    common = (flat(second), flat(grad_out), flat(row), up_weight, up_bias[None].astype(F32), down_weight)
    back, two, pulled, down_send, up_send, bias_send, back_sum = run_feed(theirs, *common)
    later = [back, two, pulled, flat(middle), flat(one), flat(gate), vectors]
    down_keep, up_keep, bias_keep, mixed, grad_middle, grad_one, grad_logit, sums = run_feed(
        mine, *common, later
    )
    mixed = to_slots(cube(mixed))
    down_part = add_low(down_keep, swap(down_send, first))
    up_part = add_low(up_keep, swap(up_send, first))
    seq_bits = bits_of("seq")
    order_a = others + seq_bits
    order_b = others[::-1] + seq_bits
    down_own = sum_over(down_part, order_a)
    up_own = sum_over(up_part, order_b)

    fields = (
        tokens,
        queries,
        keys,
        values,
        lse,
        cube(grad_one),
        cube(grad_middle),
        cube(grad_logit),
        normed,
    )
    before, small = None, 0.0
    for image in range(images):
        grads, tokens_grad, image_sums = run_attention_back(
            image, fields, vectors, weights, counts, before
        )
        before = (grads, tokens_grad)
        small = small + image_sums
    tokens_grad = to_slots(tokens_grad)
    outer = run_outer(
        theirs, flat(normed), flat(context), grads.reshape(3, rows, width), grad_one
    )
    four = outer.reshape(2, 2 * width, width)
    four = add_low(four[1], swap(four[0], first))
    third = four.shape[0] // 3
    orders = [order_a, order_b, seq_bits[:1] + others + seq_bits[1:]]
    four = jnp.concatenate(
        [sum_over(four[n * third : (n + 1) * third], orders[n]) for n in range(3)]
    )

    ratio = up_bias.shape[0] // width
    small = jnp.concatenate(
        [
            small[:5],
            sums[:3],
            back_sum,
            ordered(bias_keep, bias_send, first, 1).reshape(ratio, width),
        ]
    )
    small = jnp.sum(lax.all_gather(small, ("dp", "seq"), axis=0), axis=0)

    down_grad = ordered(down_own, swap(down_own, first), first).astype(F32)
    up_grad = ordered(up_own, swap(up_own, first), first, 1).astype(F32)
    four_other = swap(four, first)
    low, high = jnp.where(own == 0, four, four_other), jnp.where(own == 0, four_other, four)
    return (
        mixed,
        tokens_grad,
        low[:width].astype(F32),
        small[0],
        low[width:].astype(F32),
        high[:width].astype(F32),
        small[1],
        high[width:].astype(F32),
        small[7],
        up_grad,
        small[9:].reshape(-1),
        down_grad,
        small[8],
        small[2],
        small[3],
        small[5],
        small[6],
        small[4],
    )


def solution(mesh):
    rows = P("dp", "seq", None)
    in_specs = (rows, P("dp"), rows) + (P(),) * 16
    out_specs = (rows, rows) + (P(),) * 16
    return jax.shard_map(
        on_device, mesh=mesh, in_specs=in_specs, out_specs=out_specs, check_vma=False
    )
```

time: 807 us -> 506 us (0.63)
  waiting for transfers between devices: 401 us -> 157 us
  matrix products: 157 us -> 0 us
  Pallas kernels: 0 us -> 148 us
  starting transfers between devices: 20.3 us -> 72.3 us
  other arithmetic: 87.3 us -> 43 us
  blocking collectives: 74.1 us -> 41.3 us
  local copies, waits for them, and re-layouts: 45.9 us -> 21.9 us
    reduce_scatter x3 -> x0, waiting for transfers between devices: 236 us -> none  [sum_devices(): lax.psum_scatter(grad.astype(jnp.bfloat16), ('dp', 'seq'), scatter_dimens...]
    dot_general x26 -> x0, matrix products: 157 us -> none  [the longest x6 37.1 us: project(): jnp.einsum('icn,no->ico', left, right, preferred_element_type=jnp.float32)]
    pallas_call x0 -> x7, Pallas kernels: none -> 148 us  [the longest x2 65.1 us: run_feed(): pl.pallas_call(body, grid_spec=pltpu.PrefetchScalarGridSpec(num_scalar_pr...]
    ppermute x0 -> x46, waiting for transfers between devices: none -> 113 us  [swap(): lax.ppermute(field, axis, [(i, i ^ 1 << b) for i in range(lax.axis_size(a...]
    all_gather x3 -> x1, waiting for transfers between devices: 83.4 us -> 0.01 us  [on_device(): small = jnp.sum(lax.all_gather(small, ('dp', 'seq'), axis=0), axis=0)]
    psum x1 -> x0, blocking collectives: 74.1 us -> none  [on_device(): lax.psum(jnp.concatenate([piece.reshape(-1, width) for piece in small]),...]
    ppermute x0 -> x46, starting transfers between devices: none -> 59.3 us  [swap(): lax.ppermute(field, axis, [(i, i ^ 1 << b) for i in range(lax.axis_size(a...]
    all_to_all x0 -> x1, blocking collectives: none -> 41.3 us  [to_images(): return lax.all_to_all(field, 'seq', split_axis=0, concat_axis=1, tiled=True)]
  transfers between devices with their start and end apart: 10 -> 50, of which waited for: 8 -> 22; matrix products, arithmetic and copies ran while one was open for 19% -> 10% of each run, Pallas kernels for 0% -> 0%
where the time goes in v2:
time: 506 us; the launch traced here: 498 us
  waiting for transfers between devices  157 us (31%)
  Pallas kernels  148 us (29%)
  starting transfers between devices  72.3 us (14%)
  other arithmetic  43 us (8%)
  blocking collectives  41.3 us (8%)
  local copies, waits for them, and re-layouts  21.9 us (4%)
  between operations  15.5 us (3%)
    ppermute x46, waiting for transfers between devices, swap(): lax.ppermute(field, axis, [(i, i ^ 1 << b) for i in range(lax.axis_size(a...  113 us
    pallas_call x2, Pallas kernels, run_feed(): pl.pallas_call(body, grid_spec=pltpu.PrefetchScalarGridSpec(num_scalar_pr...  65.1 us
    ppermute x46, starting transfers between devices, swap(): lax.ppermute(field, axis, [(i, i ^ 1 << b) for i in range(lax.axis_size(a...  59.3 us
    pallas_call x3, Pallas kernels, run_attention_back(): pl.pallas_call(functools.partial(attention_back_kernel, image=image), gri...  51.4 us
    all_to_all x1, blocking collectives, to_images(): return lax.all_to_all(field, 'seq', split_axis=0, concat_axis=1, tiled=True)  41.3 us
    all_to_all x1, waiting for transfers between devices, to_images(): return lax.all_to_all(field, 'seq', split_axis=0, concat_axis=1, tiled=True)  30.9 us
    pallas_call x1, Pallas kernels, run_attention(): pl.pallas_call(attention_kernel, grid_spec=pltpu.PrefetchScalarGridSpec(n...  21 us
    all_to_all x2, waiting for transfers between devices, to_slots(): return lax.all_to_all(field, 'seq', split_axis=1, concat_axis=0, tiled=True)  12.8 us
  transfers between devices with their start and end apart: 50, of which 22 were waited for; matrix products, arithmetic and copies ran while one was open for 10% of the time, Pallas kernels for 0%

profile of v2, /device:TPU:0, one launch (start us, length us, event | category | flops | bytes accessed | tf_op | source)
XLA Modules:
  0.0 498.3 jit_solution(3133543028757996371)
XLA Ops:
  7.3 41.3 %all_to_all.69 = bf16[12,80,768]{2,1,0:T(8,128)(2,1)S(1)} all-to-all(bf16[12,80,768]{2,1,0:T(8,128)(2,1)} %param.19), channel_id=1, replica_groups=mesh['dp'=8,'seq'=4] {'seq'}, dimensions={0} | all-to-all | bytes 2949120 | tf_op jit(solution)/shard_map/all_to_all | solution.py:540
  48.6 3.6 all-to-all-start.1
  55.5 30.9 %all-to-all-done.1 = bf16[12,80,768]{2,1,0:T(8,128)(2,1)S(1)} async-done(((bf16[12,80,768]{2,1,0:T(8,128)(2,1)}), bf16[12,80,768]{2,1,0:T(8,128)(2,1)S(1)}, u32[]{:S(2)}, u32[]{:S(2)}) %all-to-all-start.1) | async-done | bytes 1474592 | tf_op jit(solution)/shard_map/all_to_all | solution.py:540
  87.7 21.0 %attention_forward.1 = (bf16[3,320,768]{2,1,0:T(8,128)(2,1)}, bf16[3,320,768]{2,1,0:T(8,128)(2,1)}, bf16[3,320,768]{2,1,0:T(8,128)(2,1)}, bf16[3,320,768]{2,1,0:...) custom-call(s32[3]{0:T(128)} %and_select_fusion.counts, ...), custom_call_target="tpu_custom_call" | custom-call | flops 5473566720 | bytes 40000000 | tf_op jit(solution)/shard_map/attention_forward/pallas_call | solution.py:141
  108.7 26.7 %feed_first.1 = (bf16[960,768]{1,0:T(8,128)(2,1)}, f32[960,768]{1,0:T(8,128)}, f32[960,768]{1,0:T(8,128)}, bf16[1536,768]{1,0:T(8,128)(2,1)}, bf16[768,1536]{1,0...) custom-call(s32[1]{0:T(128)} %bitcast.10.half, bf16[960,768]{1,0:T(8,128)(2,1)} %bitcast.64, ...), custom_call_target="tpu_custom_call" | custom-call | flops 13589544960 | bytes 30000000 | tf_op jit(solution)/shard_map/feed_first/pallas_call | solution.py:302
  135.4 38.4 %feed_second.1 = (bf16[1536,768]{1,0:T(8,128)(2,1)}, bf16[768,1536]{1,0:T(8,128)(2,1)}, f32[1,1536]{1,0:T(1,128)}, bf16[960,768]{1,0:T(8,128)(2,1)}, f32[960,768...) custom-call(s32[1]{0:T(128)} %bitcast.half, bf16[960,768]{1,0:T(8,128)(2,1)} %bitcast.65, ...), custom_call_target="tpu_custom_call" | custom-call | flops 13589544960 | bytes 30000000 | tf_op jit(solution)/shard_map/feed_second/pallas_call | solution.py:302
  173.8 13.6 %attention_backward.3 = (bf16[3,3,320,768]{3,2,1,0:T(8,128)(2,1)}, bf16[3,320,768]{2,1,0:T(8,128)(2,1)}, f32[8,768]{1,0:T(8,128)}) custom-call(s32[3]{0:T(128)} %and_select_fusion.counts, bf16[3,320,768]{2,1,0:T(8,128)(2,1)} %bitcast.41, bf16[3,320,768]{2,1,0:T(8,128)(2,1)} %get-tuple-element.62.q_ref, bf16[3,320,768]{2,1,0:T(8,128)(2,1)} %get-tuple-element.63.k_ref, ...), custom_call_target="tpu_custom_call" | custom-call | flops 2296381440 | bytes 12000000 | tf_op jit(solution)/shard_map/attention_backward/pallas_call | solution.py:405
  187.4 24.2 %attention_backward.4 = (bf16[3,3,320,768]{3,2,1,0:T(8,128)(2,1)}, bf16[3,320,768]{2,1,0:T(8,128)(2,1)}, f32[8,768]{1,0:T(8,128)}) custom-call(s32[3]{0:T(128)} %and_select_fusion.counts, bf16[3,320,768]{2,1,0:T(8,128)(2,1)} %bitcast.42, bf16[3,320,768]{2,1,0:T(8,128)(2,1)} %get-tuple-element.62.q_ref, ...), custom_call_target="tpu_custom_call", output_to_operand_aliasing={{0}: (15, {}), {1}: (16, {})} | custom-call | flops 2296381440 | bytes 12000000 | tf_op jit(solution)/shard_map/attention_backward/pallas_call | solution.py:405
  211.6 13.6 %attention_backward.5 = (bf16[3,3,320,768]{3,2,1,0:T(8,128)(2,1)}, bf16[3,320,768]{2,1,0:T(8,128)(2,1)}, f32[8,768]{1,0:T(8,128)}) custom-call(s32[3]{0:T(128)} %and_select_fusion.counts, bf16[3,320,768]{2,1,0:T(8,128)(2,1)} %bitcast.43, bf16[3,320,768]{2,1,0:T(8,128)(2,1)} %get-tuple-element.62.q_ref, ...), custom_call_target="tpu_custom_call", output_to_operand_aliasing={{0}: (15, {}), {1}: (16, {})} | custom-call | flops 2296381440 | bytes 12000000 | tf_op jit(solution)/shard_map/attention_backward/pallas_call | solution.py:405
  225.3 10.0 %outer.1 = bf16[4,768,768]{2,1,0:T(8,128)(2,1)} custom-call(s32[1]{0:T(128)} %bitcast.10.half, bf16[960,768]{1,0:T(8,128)(2,1)} %bitcast.45, bf16[960,768]{1,0:T(8,128)(2,1)} %bitcast.63, bf16[3,960,768]{2,1,0:T(8,128)(2,1)} %bitcast.44, bf16[960,768]{1,0:T(8,128)(2,1)} %get-tuple-element.66.grad_one), custom_call_target="tpu_custom_call" | custom-call | flops 4529848320 | bytes 15000000 | tf_op jit(solution)/shard_map/outer/pallas_call | solution.py:449
  235.3 4.1 fusion.4
  239.9 3.9 copy.47
  243.8 4.6 all-to-all-start.2
  249.6 2.3 fusion.2
  252.1 2.0 collective-permute-start.17
  254.1 1.6 collective-permute-start.9
  255.7 1.6 collective-permute-start.1
  257.3 2.3 add_convert_fusion.1
  261.2 2.3 add_convert_fusion
  264.2 25.9 %collective-permute-done.17 = bf16[256,768]{1,0:T(8,128)(2,1)S(1)} collective-permute-done((bf16[256,768]{1,0:T(8,128)(2,1)S(1)}, bf16[256,768]{1,0:T(8,128)(2,1)S(1)}, u32[]{:S(2)}, u32[]{:S(2)}) %collective-permute-start.17) | collective-permute-done | bytes 393248 | tf_op jit(solution)/shard_map/ppermute | solution.py:489
  290.3 1.6 collective-permute-start.18
  292.7 1.6 collective-permute-start.2
  294.3 5.3 %collective-permute-done.18 = bf16[128,768]{1,0:T(8,128)(2,1)S(1)} collective-permute-done((bf16[128,768]{1,0:T(8,128)(2,1)S(1)}, bf16[128,768]{1,0:T(8,128)(2,1)S(1)}, u32[]{:S(2)}, u32[]{:S(2)}) %collective-permute-start.18) | collective-permute-done | bytes 196640 | tf_op jit(solution)/shard_map/ppermute | solution.py:489
  299.7 1.6 collective-permute-start.19
  302.3 2.6 collective-permute-start.11
  305.1 3.8 collective-permute-start.20
  309.0 3.5 collective-permute-start.12
  312.5 2.8 collective-permute-start.4
  315.6 4.5 collective-permute-done.12
  320.2 2.6 collective-permute-done.4
  323.8 1.6 collective-permute-start.22
  326.2 1.8 collective-permute-start.14
  328.0 1.5 collective-permute-start.6
  330.0 2.1 collective-permute-start.23
  334.2 13.8 %collective-permute-done.23 = bf16[128,768]{1,0:T(8,128)(2,1)S(1)} collective-permute-done((bf16[128,768]{1,0:T(8,128)(2,1)S(1)}, bf16[128,768]{1,0:T(8,128)(2,1)S(1)}, u32[]{:S(2)}, u32[]{:S(2)}) %collective-permute-start.23) | collective-permute-done | bytes 196640 | tf_op jit(solution)/shard_map/ppermute | solution.py:489
  354.0 7.8 %collective-permute-done.29 = bf16[96,1536]{1,0:T(8,128)(2,1)S(1)} collective-permute-done((bf16[96,1536]{1,0:T(8,128)(2,1)S(1)}, bf16[96,1536]{1,0:T(8,128)(2,1)S(1)}, u32[]{:S(2)}, u32[]{:S(2)}) %collective-permute-start.29) | collective-permute-done | bytes 294944 | tf_op jit(solution)/shard_map/ppermute | solution.py:489
  361.9 2.5 collective-permute-start.30
  364.3 5.1 %collective-permute-done.38 = bf16[384,768]{1,0:T(8,128)(2,1)S(1)} collective-permute-done((bf16[384,768]{1,0:T(8,128)(2,1)S(1)}, bf16[384,768]{1,0:T(8,128)(2,1)S(1)}, u32[]{:S(2)}, u32[]{:S(2)}) %collective-permute-start.38) | collective-permute-done | bytes 589856 | tf_op jit(solution)/shard_map/ppermute | solution.py:489
  369.6 1.6 collective-permute-start.39
  371.3 3.6 collective-permute-start.31
  374.9 1.7 collective-permute-done.39
  376.8 7.1 %collective-permute-start.40 = (bf16[96,768]{1,0:T(8,128)(2,1)S(1)}, bf16[96,768]{1,0:T(8,128)(2,1)S(1)}, u32[]{:S(2)}, u32[]{:S(2)}) collective-permute-start(bf16[96,768]{1,0:T(8,128)(2,1)S(1)} %constant_dynamic-slice_fusion), channel_id=1, source_target_pairs={{0,2},{1,3},{2,0},{3,1},{4,6},{5,7},{6,4},{7,5},{8,10},{9,11},{10,... | collective-permute-start | bytes 442376 | tf_op jit(solution)/shard_map/ppermute | solution.py:489
  383.9 2.7 collective-permute-start.32
  386.8 4.2 collective-permute-done.40
  391.2 2.5 collective-permute-done.32
  393.9 4.9 collective-permute-done.41
  400.5 5.1 %collective-permute-done.42 = bf16[192,768]{1,0:T(8,128)(2,1)S(1)} collective-permute-done((bf16[192,768]{1,0:T(8,128)(2,1)S(1)}, bf16[192,768]{1,0:T(8,128)(2,1)S(1)}, u32[]{:S(2)}, u32[]{:S(2)}) %collective-permute-start.42) | collective-permute-done | bytes 294944 | tf_op jit(solution)/shard_map/ppermute | solution.py:489
  406.3 2.1 collective-permute-start.34
  408.3 1.6 pad_maximum_fusion
  409.9 2.5 copy.49
  412.4 4.7 all-to-all-start.3
  417.1 5.0 collective-permute-done.43
  422.6 17.5 %collective-permute-done.34 = bf16[384,1536]{1,0:T(8,128)(2,1)} collective-permute-done((bf16[384,1536]{1,0:T(8,128)(2,1)S(1)}, bf16[384,1536]{1,0:T(8,128)(2,1)}, u32[]{:S(2)}, u32[]{:S(2)}) %collective-permute-start.34) | collective-permute-done | bytes 1179680 | tf_op jit(solution)/shard_map/ppermute | solution.py:489
  440.1 2.7 maximum_select_fusion.2
  442.9 3.1 collective-permute-done.44
  446.0 1.8 maximum_select_fusion.3
  447.8 2.8 copy.48
  450.7 12.8 %all-to-all-done.3 = bf16[3,320,768]{2,0,1:T(4,128)(2,1)} async-done(((bf16[3,320,768]{2,0,1:T(4,128)(2,1)}), bf16[3,320,768]{2,0,1:T(4,128)(2,1)}, u32[]{:S(2)}, u32[]{:S(2)}) %all-to-all-start.3) | async-done | bytes 1474592 | tf_op jit(solution)/shard_map/all_to_all | solution.py:544
  463.5 2.8 copy.50
  466.4 1.5 reduce_sum.9
  469.2 2.5 broadcast_select_fusion
  471.7 3.8 slice_convert_fusion
  475.5 6.7 %fusion = f32[768,3072]{1,0:T(8,128)} fusion(bf16[768,1536]{1,0:T(8,128)(2,1)} %collective-permute-done.35, bf16[768,1536]{1,0:T(8,128)(2,1)S(1)} %maximum_select_fusion.2, pred[]{:T(512)S(6)} %eq.10), kind=kLoop, calls=%fused_computation.1 | loop fusion | flops 23592960 | bytes 14155777 | tf_op jit(solution)/shard_map/convert_element_type | solution.py:654
  482.3 8.7 %fusion.1 = f32[3072,768]{1,0:T(8,128)} fusion(bf16[1536,768]{1,0:T(8,128)(2,1)} %collective-permute-done.45, bf16[1536,768]{1,0:T(8,128)(2,1)} %maximum_select_fusion.3, pred[]{:T(512)S(6)} %eq.10), kind=kLoop, calls=%fused_computation.3 | loop fusion | flops 23592960 | bytes 14155777 | tf_op jit(solution)/shard_map/convert_element_type | solution.py:653
  (191 shorter events, 26.8 us)
Async XLA Ops:
  7.2 45.0 %copy-start.14 = (bf16[768]{0:T(1024)(128)(2,1)S(1)}, bf16[768]{0:T(1024)(128)(2,1)}, u32[]{:S(2)}) copy-start(bf16[768]{0:T(1024)(128)(2,1)} %param.23) | copy-start | bytes 4612
  7.2 45.0 %copy-start.15 = (bf16[768]{0:T(1024)(128)(2,1)S(1)}, bf16[768]{0:T(1024)(128)(2,1)}, u32[]{:S(2)}) copy-start(bf16[768]{0:T(1024)(128)(2,1)} %param.26) | copy-start | bytes 4612
  7.2 45.0 %copy-start.16 = (bf16[768]{0:T(1024)(128)(2,1)S(1)}, bf16[768]{0:T(1024)(128)(2,1)}, u32[]{:S(2)}) copy-start(bf16[768]{0:T(1024)(128)(2,1)} %param.28) | copy-start | bytes 4612
  7.2 45.0 %copy-start.17 = (bf16[768]{0:T(1024)(128)(2,1)S(1)}, bf16[768]{0:T(1024)(128)(2,1)}, u32[]{:S(2)}) copy-start(bf16[768]{0:T(1024)(128)(2,1)} %param.33) | copy-start | bytes 4612
  7.2 45.0 %copy-start.18 = (bf16[768]{0:T(1024)(128)(2,1)S(1)}, bf16[768]{0:T(1024)(128)(2,1)}, u32[]{:S(2)}) copy-start(bf16[768]{0:T(1024)(128)(2,1)} %param.34) | copy-start | bytes 4612
  7.2 45.1 %copy-start.19 = (bf16[768]{0:T(1024)(128)(2,1)S(1)}, bf16[768]{0:T(1024)(128)(2,1)}, u32[]{:S(2)}) copy-start(bf16[768]{0:T(1024)(128)(2,1)} %param.35) | copy-start | bytes 4612
  7.3 45.1 %copy-start.20 = (bf16[768]{0:T(1024)(128)(2,1)S(1)}, bf16[768]{0:T(1024)(128)(2,1)}, u32[]{:S(2)}) copy-start(bf16[768]{0:T(1024)(128)(2,1)} %param.36) | copy-start | bytes 4612
  7.3 45.1 %copy-start.21 = (bf16[768]{0:T(1024)(128)(2,1)S(1)}, bf16[768]{0:T(1024)(128)(2,1)}, u32[]{:S(2)}) copy-start(bf16[768]{0:T(1024)(128)(2,1)} %param.37) | copy-start | bytes 4612
  7.3 45.1 %copy-start.22 = (bf16[768]{0:T(1024)(128)(2,1)S(1)}, bf16[768]{0:T(1024)(128)(2,1)}, u32[]{:S(2)}) copy-start(bf16[768]{0:T(1024)(128)(2,1)} %param.32) | copy-start | bytes 4612
  7.3 45.1 %copy-start.10 = (bf16[3072]{0:T(1024)(128)(2,1)S(1)}, bf16[3072]{0:T(1024)(128)(2,1)}, u32[]{:S(2)}) copy-start(bf16[3072]{0:T(1024)(128)(2,1)} %param.30) | copy-start | bytes 18436
  7.3 45.8 %copy-start.23 = (s32[12]{0:T(128)S(1)}, s32[12]{0:T(128)}, u32[]{:S(2)}) copy-start(s32[12]{0:T(128)} %param.20) | copy-start | bytes 148
  48.6 37.8 %all-to-all-start.1 = ((bf16[12,80,768]{2,1,0:T(8,128)(2,1)}), bf16[12,80,768]{2,1,0:T(8,128)(2,1)S(1)}, u32[]{:S(2)}, u32[]{:S(2)}) async-start(bf16[12,80,768]{2,1,0:T(8,128)(2,1)} %param.21), calls=%async_computation.1 | async-start | bytes 2949120 | tf_op jit(solution)/shard_map/all_to_all | solution.py:540
  239.4 10.2 %collective-permute-start = (bf16[1536,768]{1,0:T(8,128)(2,1)}, bf16[1536,768]{1,0:T(8,128)(2,1)}, u32[]{:S(2)}, u32[]{:S(2)}) collective-permute-start(bf16[1536,768]{1,0:T(8,128)(2,1)} %bitcast.30), channel_id=1, source_target_pairs={{0,4},{4,0},{8,12},{12,8},{16,20},{20,16},{24,28},{28,24},{1,5},{5... | collective-permute-start | bytes 7077896 | tf_op jit(solution)/shard_map/ppermute | solution.py:489
  239.4 17.9 %collective-permute-start.26 = (bf16[768,1536]{1,0:T(8,128)(2,1)}, bf16[768,1536]{1,0:T(8,128)(2,1)}, u32[]{:S(2)}, u32[]{:S(2)}) collective-permute-start(bf16[768,1536]{1,0:T(8,128)(2,1)} %get-tuple-element.85), channel_id=1, source_target_pairs={{0,4},{4,0},{8,12},{12,8},{16,20},{20,16},{24,28},{28,24},{1,5},{5... | collective-permute-start | bytes 7077896 | tf_op jit(solution)/shard_map/ppermute | solution.py:489
  243.8 168.6 %all-to-all-start.2 = ((bf16[3,320,768]{2,0,1:T(4,128)(2,1)}), bf16[3,320,768]{2,0,1:T(4,128)(2,1)}, u32[]{:S(2)}, u32[]{:S(2)}) async-start(bf16[3,320,768]{2,0,1:T(4,128)(2,1)} %copy.47), calls=%async_computation.2 | async-start | bytes 3932160 | tf_op jit(solution)/shard_map/all_to_all | solution.py:544
  248.4 217.9 %all-gather.4.cloned.1.call-start = ((), (), s32[]{:S(2)}) async-start(), calls=%async_computation.4 | async-start | bytes 1622016 | tf_op jit(solution)/shard_map/all_gather | solution.py:651
  248.8 11.5 %collective-permute-start.36 = (bf16[1536,768]{1,0:T(8,128)(2,1)}, bf16[1536,768]{1,0:T(8,128)(2,1)}, u32[]{:S(2)}, u32[]{:S(2)}) collective-permute-start(bf16[1536,768]{1,0:T(8,128)(2,1)} %get-tuple-element.87), channel_id=1, source_target_pairs={{0,4},{4,0},{8,12},{12,8},{16,20},{20,16},{24,28},{28,24},{1,5},{5... | collective-permute-start | bytes 7077896 | tf_op jit(solution)/shard_map/ppermute | solution.py:489
  252.0 5.3 %copy-start.5 = (bf16[768,1536]{1,0:T(8,128)(2,1)S(1)}, bf16[768,1536]{1,0:T(8,128)(2,1)}, u32[]{:S(2)}) copy-start(bf16[768,1536]{1,0:T(8,128)(2,1)} %get-tuple-element.84) | copy-start | bytes 7077892
  252.1 38.1 %collective-permute-start.17 = (bf16[256,768]{1,0:T(8,128)(2,1)S(1)}, bf16[256,768]{1,0:T(8,128)(2,1)S(1)}, u32[]{:S(2)}, u32[]{:S(2)}) collective-permute-start(bf16[256,768]{1,0:T(8,128)(2,1)S(1)} %constant_dynamic-slice_fusion.11), channel_id=1, source_target_pairs={{0,1},{1,0},{2,3},{3,2},{4,5},{5,4},{6,7},{7,6},{8,9},{9,8},{10,11... | collective-permute-start | bytes 1179656 | tf_op jit(solution)/shard_map/ppermute | solution.py:489
  254.1 37.7 %collective-permute-start.9 = (bf16[256,768]{1,0:T(8,128)(2,1)S(1)}, bf16[256,768]{1,0:T(8,128)(2,1)S(1)}, u32[]{:S(2)}, u32[]{:S(2)}) collective-permute-start(bf16[256,768]{1,0:T(8,128)(2,1)S(1)} %constant_dynamic-slice_fusion.15), channel_id=1, source_target_pairs={{0,16},{4,20},{8,24},{12,28},{16,0},{20,4},{24,8},{28,12},{1,17},{... | collective-permute-start | bytes 1179656 | tf_op jit(solution)/shard_map/ppermute | solution.py:489
  255.7 36.9 %collective-permute-start.1 = (bf16[256,768]{1,0:T(8,128)(2,1)S(1)}, bf16[256,768]{1,0:T(8,128)(2,1)S(1)}, u32[]{:S(2)}, u32[]{:S(2)}) collective-permute-start(bf16[256,768]{1,0:T(8,128)(2,1)S(1)} %constant_dynamic-slice_fusion.19), channel_id=1, source_target_pairs={{0,8},{4,12},{8,0},{12,4},{16,24},{20,28},{24,16},{28,20},{1,9},{5... | collective-permute-start | bytes 1179656 | tf_op jit(solution)/shard_map/ppermute | solution.py:489
  259.7 69.9 %collective-permute-start.27 = (bf16[384,1536]{1,0:T(8,128)(2,1)S(1)}, bf16[384,1536]{1,0:T(8,128)(2,1)S(1)}, u32[]{:S(2)}, u32[]{:S(2)}) collective-permute-start(bf16[384,1536]{1,0:T(8,128)(2,1)S(1)} %constant_dynamic-slice_fusion.7), channel_id=1, source_target_pairs={{0,16},{4,20},{8,24},{12,28},{16,0},{20,4},{24,8},{28,12},{1,17},{... | collective-permute-start | bytes 3538952 | tf_op jit(solution)/shard_map/ppermute | solution.py:489
  263.6 88.9 %collective-permute-start.37 = (bf16[768,768]{1,0:T(8,128)(2,1)S(1)}, bf16[768,768]{1,0:T(8,128)(2,1)S(1)}, u32[]{:S(2)}, u32[]{:S(2)}) collective-permute-start(bf16[768,768]{1,0:T(8,128)(2,1)S(1)} %constant_dynamic-slice_fusion.3), channel_id=1, source_target_pairs={{0,8},{4,12},{8,0},{12,4},{16,24},{20,28},{24,16},{28,20},{1,9},{5... | collective-permute-start | bytes 3538952 | tf_op jit(solution)/shard_map/ppermute | solution.py:489
  290.3 9.3 %collective-permute-start.18 = (bf16[128,768]{1,0:T(8,128)(2,1)S(1)}, bf16[128,768]{1,0:T(8,128)(2,1)S(1)}, u32[]{:S(2)}, u32[]{:S(2)}) collective-permute-start(bf16[128,768]{1,0:T(8,128)(2,1)S(1)} %constant_dynamic-slice_fusion.10), channel_id=1, source_target_pairs={{0,8},{4,12},{8,0},{12,4},{16,24},{20,28},{24,16},{28,20},{1,9},{5... | collective-permute-start | bytes 589832 | tf_op jit(solution)/shard_map/ppermute | solution.py:489
  292.0 10.3 %collective-permute-start.10 = (bf16[128,768]{1,0:T(8,128)(2,1)S(1)}, bf16[128,768]{1,0:T(8,128)(2,1)S(1)}, u32[]{:S(2)}, u32[]{:S(2)}) collective-permute-start(bf16[128,768]{1,0:T(8,128)(2,1)S(1)} %constant_dynamic-slice_fusion.14), channel_id=1, source_target_pairs={{0,8},{4,12},{8,0},{12,4},{16,24},{20,28},{24,16},{28,20},{1,9},{5... | collective-permute-start | bytes 589832 | tf_op jit(solution)/shard_map/ppermute | solution.py:489
  292.7 12.2 %collective-permute-start.2 = (bf16[128,768]{1,0:T(8,128)(2,1)S(1)}, bf16[128,768]{1,0:T(8,128)(2,1)S(1)}, u32[]{:S(2)}, u32[]{:S(2)}) collective-permute-start(bf16[128,768]{1,0:T(8,128)(2,1)S(1)} %constant_dynamic-slice_fusion.18), channel_id=1, source_target_pairs={{0,16},{4,20},{8,24},{12,28},{16,0},{20,4},{24,8},{28,12},{1,17},{... | collective-permute-start | bytes 589832 | tf_op jit(solution)/shard_map/ppermute | solution.py:489
  299.7 5.4 %collective-permute-start.19 = (bf16[64,768]{1,0:T(8,128)(2,1)S(1)}, bf16[64,768]{1,0:T(8,128)(2,1)S(1)}, u32[]{:S(2)}, u32[]{:S(2)}) collective-permute-start(bf16[64,768]{1,0:T(8,128)(2,1)S(1)} %constant_dynamic-slice_fusion.9), channel_id=1, source_target_pairs={{0,16},{4,20},{8,24},{12,28},{16,0},{20,4},{24,8},{28,12},{1,17},{... | collective-permute-start | bytes 294920 | tf_op jit(solution)/shard_map/ppermute | solution.py:489
  302.3 6.6 %collective-permute-start.11 = (bf16[64,768]{1,0:T(8,128)(2,1)S(1)}, bf16[64,768]{1,0:T(8,128)(2,1)S(1)}, u32[]{:S(2)}, u32[]{:S(2)}) collective-permute-start(bf16[64,768]{1,0:T(8,128)(2,1)S(1)} %constant_dynamic-slice_fusion.13), channel_id=1, source_target_pairs={{0,1},{1,0},{2,3},{3,2},{4,5},{5,4},{6,7},{7,6},{8,9},{9,8},{10,11... | collective-permute-start | bytes 294920 | tf_op jit(solution)/shard_map/ppermute | solution.py:489
  305.0 7.5 %collective-permute-start.3 = (bf16[64,768]{1,0:T(8,128)(2,1)S(1)}, bf16[64,768]{1,0:T(8,128)(2,1)S(1)}, u32[]{:S(2)}, u32[]{:S(2)}) collective-permute-start(bf16[64,768]{1,0:T(8,128)(2,1)S(1)} %constant_dynamic-slice_fusion.17), channel_id=1, source_target_pairs={{0,1},{1,0},{2,3},{3,2},{4,5},{5,4},{6,7},{7,6},{8,9},{9,8},{10,11... | collective-permute-start | bytes 294920 | tf_op jit(solution)/shard_map/ppermute | solution.py:489
  305.1 10.2 %collective-permute-start.20 = (bf16[32,768]{1,0:T(8,128)(2,1)S(1)}, bf16[32,768]{1,0:T(8,128)(2,1)S(1)}, u32[]{:S(2)}, u32[]{:S(2)}) collective-permute-start(bf16[32,768]{1,0:T(8,128)(2,1)S(1)} %constant_dynamic-slice_fusion.8), channel_id=1, source_target_pairs={{0,2},{1,3},{2,0},{3,1},{4,6},{5,7},{6,4},{7,5},{8,10},{9,11},{10,... | collective-permute-start | bytes 147464 | tf_op jit(solution)/shard_map/ppermute | solution.py:489
  309.0 11.1 %collective-permute-start.12 = (bf16[32,768]{1,0:T(8,128)(2,1)S(1)}, bf16[32,768]{1,0:T(8,128)(2,1)S(1)}, u32[]{:S(2)}, u32[]{:S(2)}) collective-permute-start(bf16[32,768]{1,0:T(8,128)(2,1)S(1)} %constant_dynamic-slice_fusion.12), channel_id=1, source_target_pairs={{0,2},{1,3},{2,0},{3,1},{4,6},{5,7},{6,4},{7,5},{8,10},{9,11},{10,... | collective-permute-start | bytes 147464 | tf_op jit(solution)/shard_map/ppermute | solution.py:489
  312.5 10.3 %collective-permute-start.4 = (bf16[32,768]{1,0:T(8,128)(2,1)S(1)}, bf16[32,768]{1,0:T(8,128)(2,1)S(1)}, u32[]{:S(2)}, u32[]{:S(2)}) collective-permute-start(bf16[32,768]{1,0:T(8,128)(2,1)S(1)} %constant_dynamic-slice_fusion.16), channel_id=1, source_target_pairs={{0,2},{1,3},{2,0},{3,1},{4,6},{5,7},{6,4},{7,5},{8,10},{9,11},{10,... | collective-permute-start | bytes 147464 | tf_op jit(solution)/shard_map/ppermute | solution.py:489
  315.3 8.5 %collective-permute-start.21 = (bf16[32,768]{1,0:T(8,128)(2,1)S(1)}, bf16[32,768]{1,0:T(8,128)(2,1)S(1)}, u32[]{:S(2)}, u32[]{:S(2)}) collective-permute-start(bf16[32,768]{1,0:T(8,128)(2,1)S(1)} %add_convert_fusion.19), channel_id=1, source_target_pairs={{0,2},{1,3},{2,0},{3,1},{4,6},{5,7},{6,4},{7,5},{8,10},{9,11},{10,... | collective-permute-start | bytes 147464 | tf_op jit(solution)/shard_map/ppermute | solution.py:489
  320.1 6.1 %collective-permute-start.13 = (bf16[32,768]{1,0:T(8,128)(2,1)S(1)}, bf16[32,768]{1,0:T(8,128)(2,1)S(1)}, u32[]{:S(2)}, u32[]{:S(2)}) collective-permute-start(bf16[32,768]{1,0:T(8,128)(2,1)S(1)} %add_convert_fusion.20), channel_id=1, source_target_pairs={{0,2},{1,3},{2,0},{3,1},{4,6},{5,7},{6,4},{7,5},{8,10},{9,11},{10,... | collective-permute-start | bytes 147464 | tf_op jit(solution)/shard_map/ppermute | solution.py:489
  322.8 5.2 %collective-permute-start.5 = (bf16[32,768]{1,0:T(8,128)(2,1)S(1)}, bf16[32,768]{1,0:T(8,128)(2,1)S(1)}, u32[]{:S(2)}, u32[]{:S(2)}) collective-permute-start(bf16[32,768]{1,0:T(8,128)(2,1)S(1)} %add_convert_fusion.21), channel_id=1, source_target_pairs={{0,2},{1,3},{2,0},{3,1},{4,6},{5,7},{6,4},{7,5},{8,10},{9,11},{10,... | collective-permute-start | bytes 147464 | tf_op jit(solution)/shard_map/ppermute | solution.py:489
  323.8 6.1 %collective-permute-start.22 = (bf16[64,768]{1,0:T(8,128)(2,1)S(1)}, bf16[64,768]{1,0:T(8,128)(2,1)S(1)}, u32[]{:S(2)}, u32[]{:S(2)}) collective-permute-start(bf16[64,768]{1,0:T(8,128)(2,1)S(1)} %maximum_select_fusion.21), channel_id=1, source_target_pairs={{0,16},{4,20},{8,24},{12,28},{16,0},{20,4},{24,8},{28,12},{1,17},{... | collective-permute-start | bytes 294920 | tf_op jit(solution)/shard_map/ppermute | solution.py:489
  326.2 5.9 %collective-permute-start.14 = (bf16[64,768]{1,0:T(8,128)(2,1)S(1)}, bf16[64,768]{1,0:T(8,128)(2,1)S(1)}, u32[]{:S(2)}, u32[]{:S(2)}) collective-permute-start(bf16[64,768]{1,0:T(8,128)(2,1)S(1)} %maximum_select_fusion.20), channel_id=1, source_target_pairs={{0,1},{1,0},{2,3},{3,2},{4,5},{5,4},{6,7},{7,6},{8,9},{9,8},{10,11... | collective-permute-start | bytes 294920 | tf_op jit(solution)/shard_map/ppermute | solution.py:489
  328.0 4.7 collective-permute-start.6
  329.9 21.7 %collective-permute-start.28 = (bf16[192,1536]{1,0:T(8,128)(2,1)S(1)}, bf16[192,1536]{1,0:T(8,128)(2,1)S(1)}, u32[]{:S(2)}, u32[]{:S(2)}) collective-permute-start(bf16[192,1536]{1,0:T(8,128)(2,1)S(1)} %constant_dynamic-slice_fusion.6), channel_id=1, source_target_pairs={{0,8},{4,12},{8,0},{12,4},{16,24},{20,28},{24,16},{28,20},{1,9},{5... | collective-permute-start | bytes 1769480 | tf_op jit(solution)/shard_map/ppermute | solution.py:489
  330.0 17.9 %collective-permute-start.23 = (bf16[128,768]{1,0:T(8,128)(2,1)S(1)}, bf16[128,768]{1,0:T(8,128)(2,1)S(1)}, u32[]{:S(2)}, u32[]{:S(2)}) collective-permute-start(bf16[128,768]{1,0:T(8,128)(2,1)S(1)} %maximum_select_fusion.18), channel_id=1, source_target_pairs={{0,8},{4,12},{8,0},{12,4},{16,24},{20,28},{24,16},{28,20},{1,9},{5... | collective-permute-start | bytes 589832 | tf_op jit(solution)/shard_map/ppermute | solution.py:489
  332.1 17.9 %collective-permute-start.15 = (bf16[128,768]{1,0:T(8,128)(2,1)S(1)}, bf16[128,768]{1,0:T(8,128)(2,1)S(1)}, u32[]{:S(2)}, u32[]{:S(2)}) collective-permute-start(bf16[128,768]{1,0:T(8,128)(2,1)S(1)} %maximum_select_fusion.17), channel_id=1, source_target_pairs={{0,8},{4,12},{8,0},{12,4},{16,24},{20,28},{24,16},{28,20},{1,9},{5... | collective-permute-start | bytes 589832 | tf_op jit(solution)/shard_map/ppermute | solution.py:489
  332.7 53.9 %collective-permute-start.7 = (bf16[128,768]{1,0:T(8,128)(2,1)S(1)}, bf16[128,768]{1,0:T(8,128)(2,1)S(1)}, u32[]{:S(2)}, u32[]{:S(2)}) collective-permute-start(bf16[128,768]{1,0:T(8,128)(2,1)S(1)} %maximum_select_fusion.16), channel_id=1, source_target_pairs={{0,16},{4,20},{8,24},{12,28},{16,0},{20,4},{24,8},{28,12},{1,17},{... | collective-permute-start | bytes 589832 | tf_op jit(solution)/shard_map/ppermute | solution.py:489
  348.1 51.4 %collective-permute-start.24 = (bf16[256,768]{1,0:T(8,128)(2,1)S(1)}, bf16[256,768]{1,0:T(8,128)(2,1)S(1)}, u32[]{:S(2)}, u32[]{:S(2)}) collective-permute-start(bf16[256,768]{1,0:T(8,128)(2,1)S(1)} %maximum_select_fusion.13), channel_id=1, source_target_pairs={{0,1},{1,0},{2,3},{3,2},{4,5},{5,4},{6,7},{7,6},{8,9},{9,8},{10,11... | collective-permute-start | bytes 1179656 | tf_op jit(solution)/shard_map/ppermute | solution.py:489
  350.2 49.6 %collective-permute-start.16 = (bf16[256,768]{1,0:T(8,128)(2,1)S(1)}, bf16[256,768]{1,0:T(8,128)(2,1)S(1)}, u32[]{:S(2)}, u32[]{:S(2)}) collective-permute-start(bf16[256,768]{1,0:T(8,128)(2,1)S(1)} %maximum_select_fusion.12), channel_id=1, source_target_pairs={{0,16},{4,20},{8,24},{12,28},{16,0},{20,4},{24,8},{28,12},{1,17},{... | collective-permute-start | bytes 1179656 | tf_op jit(solution)/shard_map/ppermute | solution.py:489
  351.8 9.9 %collective-permute-start.29 = (bf16[96,1536]{1,0:T(8,128)(2,1)S(1)}, bf16[96,1536]{1,0:T(8,128)(2,1)S(1)}, u32[]{:S(2)}, u32[]{:S(2)}) collective-permute-start(bf16[96,1536]{1,0:T(8,128)(2,1)S(1)} %constant_dynamic-slice_fusion.5), channel_id=1, source_target_pairs={{0,1},{1,0},{2,3},{3,2},{4,5},{5,4},{6,7},{7,6},{8,9},{9,8},{10,11... | collective-permute-start | bytes 884744 | tf_op jit(solution)/shard_map/ppermute | solution.py:489
  352.8 16.6 %collective-permute-start.38 = (bf16[384,768]{1,0:T(8,128)(2,1)S(1)}, bf16[384,768]{1,0:T(8,128)(2,1)S(1)}, u32[]{:S(2)}, u32[]{:S(2)}) collective-permute-start(bf16[384,768]{1,0:T(8,128)(2,1)S(1)} %constant_dynamic-slice_fusion.2), channel_id=1, source_target_pairs={{0,16},{4,20},{8,24},{12,28},{16,0},{20,4},{24,8},{28,12},{1,17},{... | collective-permute-start | bytes 1769480 | tf_op jit(solution)/shard_map/ppermute | solution.py:489
  361.9 9.4 %collective-permute-start.30 = (bf16[48,1536]{1,0:T(8,128)(2,1)S(1)}, bf16[48,1536]{1,0:T(8,128)(2,1)S(1)}, u32[]{:S(2)}, u32[]{:S(2)}) collective-permute-start(bf16[48,1536]{1,0:T(8,128)(2,1)S(1)} %constant_dynamic-slice_fusion.4), channel_id=1, source_target_pairs={{0,2},{1,3},{2,0},{3,1},{4,6},{5,7},{6,4},{7,5},{8,10},{9,11},{10,... | collective-permute-start | bytes 442376 | tf_op jit(solution)/shard_map/ppermute | solution.py:489
  369.6 7.0 %collective-permute-start.39 = (bf16[192,768]{1,0:T(8,128)(2,1)S(1)}, bf16[192,768]{1,0:T(8,128)(2,1)S(1)}, u32[]{:S(2)}, u32[]{:S(2)}) collective-permute-start(bf16[192,768]{1,0:T(8,128)(2,1)S(1)} %constant_dynamic-slice_fusion.1), channel_id=1, source_target_pairs={{0,1},{1,0},{2,3},{3,2},{4,5},{5,4},{6,7},{7,6},{8,9},{9,8},{10,11... | collective-permute-start | bytes 884744 | tf_op jit(solution)/shard_map/ppermute | solution.py:489
  371.3 12.6 %collective-permute-start.31 = (bf16[48,1536]{1,0:T(8,128)(2,1)S(1)}, bf16[48,1536]{1,0:T(8,128)(2,1)S(1)}, u32[]{:S(2)}, u32[]{:S(2)}) collective-permute-start(bf16[48,1536]{1,0:T(8,128)(2,1)S(1)} %add_convert_fusion.15), channel_id=1, source_target_pairs={{0,2},{1,3},{2,0},{3,1},{4,6},{5,7},{6,4},{7,5},{8,10},{9,11},{10,... | collective-permute-start | bytes 442376 | tf_op jit(solution)/shard_map/ppermute | solution.py:489
  376.8 14.3 %collective-permute-start.40 = (bf16[96,768]{1,0:T(8,128)(2,1)S(1)}, bf16[96,768]{1,0:T(8,128)(2,1)S(1)}, u32[]{:S(2)}, u32[]{:S(2)}) collective-permute-start(bf16[96,768]{1,0:T(8,128)(2,1)S(1)} %constant_dynamic-slice_fusion), channel_id=1, source_target_pairs={{0,2},{1,3},{2,0},{3,1},{4,6},{5,7},{6,4},{7,5},{8,10},{9,11},{10,... | collective-permute-start | bytes 442376 | tf_op jit(solution)/shard_map/ppermute | solution.py:489
  383.9 9.7 %collective-permute-start.32 = (bf16[96,1536]{1,0:T(8,128)(2,1)S(1)}, bf16[96,1536]{1,0:T(8,128)(2,1)S(1)}, u32[]{:S(2)}, u32[]{:S(2)}) collective-permute-start(bf16[96,1536]{1,0:T(8,128)(2,1)S(1)} %maximum_select_fusion.14), channel_id=1, source_target_pairs={{0,1},{1,0},{2,3},{3,2},{4,5},{5,4},{6,7},{7,6},{8,9},{9,8},{10,11... | collective-permute-start | bytes 884744 | tf_op jit(solution)/shard_map/ppermute | solution.py:489
  386.7 13.4 %collective-permute-start.8 = (bf16[256,768]{1,0:T(8,128)(2,1)S(1)}, bf16[256,768]{1,0:T(8,128)(2,1)S(1)}, u32[]{:S(2)}, u32[]{:S(2)}) collective-permute-start(bf16[256,768]{1,0:T(8,128)(2,1)S(1)} %maximum_select_fusion.11), channel_id=1, source_target_pairs={{0,8},{4,12},{8,0},{12,4},{16,24},{20,28},{24,16},{28,20},{1,9},{5... | collective-permute-start | bytes 1179656 | tf_op jit(solution)/shard_map/ppermute | solution.py:489
  391.1 7.7 %collective-permute-start.41 = (bf16[96,768]{1,0:T(8,128)(2,1)S(1)}, bf16[96,768]{1,0:T(8,128)(2,1)S(1)}, u32[]{:S(2)}, u32[]{:S(2)}) collective-permute-start(bf16[96,768]{1,0:T(8,128)(2,1)S(1)} %add_convert_fusion.14), channel_id=1, source_target_pairs={{0,2},{1,3},{2,0},{3,1},{4,6},{5,7},{6,4},{7,5},{8,10},{9,11},{10,... | collective-permute-start | bytes 442376 | tf_op jit(solution)/shard_map/ppermute | solution.py:489
  393.8 12.1 %collective-permute-start.33 = (bf16[192,1536]{1,0:T(8,128)(2,1)S(1)}, bf16[192,1536]{1,0:T(8,128)(2,1)S(1)}, u32[]{:S(2)}, u32[]{:S(2)}) collective-permute-start(bf16[192,1536]{1,0:T(8,128)(2,1)S(1)} %maximum_select_fusion.9), channel_id=1, source_target_pairs={{0,8},{4,12},{8,0},{12,4},{16,24},{20,28},{24,16},{28,20},{1,9},{5... | collective-permute-start | bytes 1769480 | tf_op jit(solution)/shard_map/ppermute | solution.py:489
  398.8 6.8 %collective-permute-start.42 = (bf16[192,768]{1,0:T(8,128)(2,1)S(1)}, bf16[192,768]{1,0:T(8,128)(2,1)S(1)}, u32[]{:S(2)}, u32[]{:S(2)}) collective-permute-start(bf16[192,768]{1,0:T(8,128)(2,1)S(1)} %maximum_select_fusion.15), channel_id=1, source_target_pairs={{0,1},{1,0},{2,3},{3,2},{4,5},{5,4},{6,7},{7,6},{8,9},{9,8},{10,11... | collective-permute-start | bytes 884744 | tf_op jit(solution)/shard_map/ppermute | solution.py:489
  400.1 8.2 %copy-start.1 = (bf16[512,768]{1,0:T(8,128)(2,1)}, bf16[512,768]{1,0:T(8,128)(2,1)S(1)}, u32[]{:S(2)}) copy-start(bf16[512,768]{1,0:T(8,128)(2,1)S(1)} %maximum_select_fusion.7) | copy-start | bytes 2359300
  400.4 9.4 %copy-start.2 = (bf16[512,768]{1,0:T(8,128)(2,1)}, bf16[512,768]{1,0:T(8,128)(2,1)S(1)}, u32[]{:S(2)}) copy-start(bf16[512,768]{1,0:T(8,128)(2,1)S(1)} %maximum_select_fusion.6) | copy-start | bytes 2359300
  405.8 16.3 %collective-permute-start.43 = (bf16[384,768]{1,0:T(8,128)(2,1)S(1)}, bf16[384,768]{1,0:T(8,128)(2,1)S(1)}, u32[]{:S(2)}, u32[]{:S(2)}) collective-permute-start(bf16[384,768]{1,0:T(8,128)(2,1)S(1)} %maximum_select_fusion.10), channel_id=1, source_target_pairs={{0,16},{4,20},{8,24},{12,28},{16,0},{20,4},{24,8},{28,12},{1,17},{... | collective-permute-start | bytes 1769480 | tf_op jit(solution)/shard_map/ppermute | solution.py:489
  406.3 33.9 %collective-permute-start.34 = (bf16[384,1536]{1,0:T(8,128)(2,1)S(1)}, bf16[384,1536]{1,0:T(8,128)(2,1)}, u32[]{:S(2)}, u32[]{:S(2)}) collective-permute-start(bf16[384,1536]{1,0:T(8,128)(2,1)S(1)} %maximum_select_fusion.4), channel_id=1, source_target_pairs={{0,16},{4,20},{8,24},{12,28},{16,0},{20,4},{24,8},{28,12},{1,17},{... | collective-permute-start | bytes 3538952 | tf_op jit(solution)/shard_map/ppermute | solution.py:489
  409.9 59.3 %collective-permute-start.25 = (bf16[1536,768]{1,0:T(8,128)(2,1)}, bf16[1536,768]{1,0:T(8,128)(2,1)}, u32[]{:S(2)}, u32[]{:S(2)}) collective-permute-start(bf16[1536,768]{1,0:T(8,128)(2,1)} %pad_maximum_fusion), channel_id=1, source_target_pairs={{0,4},{4,0},{8,12},{12,8},{16,20},{20,16},{24,28},{28,24},{1,5},{5... | collective-permute-start | bytes 7077896 | tf_op jit(solution)/shard_map/ppermute | solution.py:489
  412.4 51.1 %all-to-all-start.3 = ((bf16[3,320,768]{2,0,1:T(4,128)(2,1)}), bf16[3,320,768]{2,0,1:T(4,128)(2,1)}, u32[]{:S(2)}, u32[]{:S(2)}) async-start(bf16[3,320,768]{2,0,1:T(4,128)(2,1)} %copy.49), calls=%async_computation.3 | async-start | bytes 3932160 | tf_op jit(solution)/shard_map/all_to_all | solution.py:544
  422.6 23.5 %collective-permute-start.44 = (bf16[768,768]{1,0:T(8,128)(2,1)S(1)}, bf16[768,768]{1,0:T(8,128)(2,1)S(1)}, u32[]{:S(2)}, u32[]{:S(2)}) collective-permute-start(bf16[768,768]{1,0:T(8,128)(2,1)S(1)} %maximum_select_fusion.5), channel_id=1, source_target_pairs={{0,8},{4,12},{8,0},{12,4},{16,24},{20,28},{24,16},{28,20},{1,9},{5... | collective-permute-start | bytes 3538952 | tf_op jit(solution)/shard_map/ppermute | solution.py:489
  442.8 32.7 %collective-permute-start.35 = (bf16[768,1536]{1,0:T(8,128)(2,1)S(1)}, bf16[768,1536]{1,0:T(8,128)(2,1)}, u32[]{:S(2)}, u32[]{:S(2)}) collective-permute-start(bf16[768,1536]{1,0:T(8,128)(2,1)S(1)} %maximum_select_fusion.2), channel_id=1, source_target_pairs={{0,4},{4,0},{8,12},{12,8},{16,20},{20,16},{24,28},{28,24},{1,5},{5... | collective-permute-start | bytes 7077896 | tf_op jit(solution)/shard_map/ppermute | solution.py:489
  447.8 34.5 %collective-permute-start.45 = (bf16[1536,768]{1,0:T(8,128)(2,1)}, bf16[1536,768]{1,0:T(8,128)(2,1)}, u32[]{:S(2)}, u32[]{:S(2)}) collective-permute-start(bf16[1536,768]{1,0:T(8,128)(2,1)} %maximum_select_fusion.3), channel_id=1, source_target_pairs={{0,4},{4,0},{8,12},{12,8},{16,20},{20,16},{24,28},{28,24},{1,5},{5... | collective-permute-start | bytes 7077896 | tf_op jit(solution)/shard_map/ppermute | solution.py:489
  (10 other events, 44.2 us)
Sparse Core Ops, SparseCore 0:
  252.1 72.0 all-gather.3
